TPU v7x, 32 devices: a whole 2x2x4 slice. The times are simulated.
32 devices in a mesh: groups: 2 (over y), space: 8 (over z, x), tm: 2 (over core).
Axes of the slice: x: 2, y: 2, z: 4, core: 2. Of those that a mesh axis runs over, the one named last changes fastest.
Arguments:
- latents: bfloat16 [4, 16, 4, 256, 256], P('groups', 'space', 'tm'), parts along dimension 0, may hold values from -6 to 6
- cotangent: bfloat16 [4, 16, 4, 256, 256], P('groups', 'space', 'tm'), parts along dimension 0, may hold values from -6 to 6
- valid_frames: int32 [4], P('groups'), parts along dimension 0, may hold values from 1 to 16, as said below
- spatial_weight: bfloat16 [9, 256, 256], replicated, may hold values from -0.125 to 0.125
- temporal_weight: bfloat16 [3, 256, 256], replicated, may hold values from -0.21875 to 0.21875
- cond_weight: bfloat16 [256, 256], replicated, may hold values from -0.375 to 0.375
Outputs:
- output: bfloat16 [4, 16, 4, 256, 256], P('groups', 'space', 'tm'), parts along dimension 0
- grad_latents: bfloat16 [4, 16, 4, 256, 256], P('groups', 'space', 'tm'), parts along dimension 0
- grad_spatial: bfloat16 [18, 256, 256], P('groups'), parts along dimension 0
- grad_temporal: bfloat16 [6, 256, 256], P('groups'), parts along dimension 0
- grad_cond: bfloat16 [512, 256], P('groups'), parts along dimension 0
There are 2 independent parts, one for each index of `groups`. A program takes and returns all parts, laid end to end along the dimension named above; an argument that names none is the same for every part. Nothing has to cross between parts.
Inputs may be any that keep to these rules, and one draw needn't show every extreme that they name: `valid_frames`: the first clip has all 16 frames valid; the others have 1 to 16.
All inputs are finite; a program needn't handle non-finite values.
Results may differ from a plain program's by a relative error of at most 0.0055.
Values may be sent and summed in bfloat16 or wider, within the bound.
A program may use at most 128 MiB of HBM per device.

v0:
```python
import jax
import jax.numpy as jnp
from jax import lax
from jax.sharding import PartitionSpec as P


def from_root(block, axis, source):
    block = jnp.where(lax.axis_index(axis) == source, block, jnp.zeros_like(block))
    return lax.psum(block, axis)


def shifted(value, axis, by):
    count = lax.axis_size(axis)
    pairs = [(i, i + by) for i in range(count) if 0 <= i + by < count]
    return lax.ppermute(value, axis, pairs)


def spatial_sum(padded, weights, flip):
    rows = padded.shape[2] - 2
    cols = padded.shape[3] - 2
    total = jnp.zeros(padded.shape[:2] + (rows, cols, weights.shape[2]), jnp.float32)
    for row_off in range(3):
        for col_off in range(3):
            if flip:
                piece = padded[
                    :, :, 2 - row_off : 2 - row_off + rows, 2 - col_off : 2 - col_off + cols
                ]
                kernel = weights[3 * row_off + col_off].T
            else:
                piece = padded[:, :, row_off : row_off + rows, col_off : col_off + cols]
                kernel = weights[3 * row_off + col_off]
            total = total + jnp.dot(piece, kernel, preferred_element_type=jnp.float32)
    return total


def lag_forward(padded_act, weights, count):
    total = 0.0
    for lag in range(3):
        total = total + jnp.dot(
            padded_act[:, 2 - lag : 2 - lag + count],
            weights[lag],
            preferred_element_type=jnp.float32,
        )
    return total


def lag_backward(padded_cot, weights, count):
    total = 0.0
    for lag in range(3):
        total = total + jnp.dot(
            padded_cot[:, lag : lag + count], weights[lag].T, preferred_element_type=jnp.float32
        )
    return total


def lag_grads(padded_act, cot, count):
    dims = (((0, 1, 2, 3), (0, 1, 2, 3)), ((), ()))
    terms = []
    for lag in range(3):
        terms.append(
            lax.dot_general(
                padded_act[:, 2 - lag : 2 - lag + count],
                cot,
                dims,
                preferred_element_type=jnp.float32,
            )
        )
    return jnp.stack(terms)


def own_window(whole, rows):
    padded_rows = jnp.pad(whole, ((0, 0), (0, 0), (1, 1), (0, 0), (0, 0)))
    start = lax.axis_index("tm") * rows
    return lax.dynamic_slice_in_dim(padded_rows, start, rows + 2, 2)


def on_device(latents, cotangent, valid_frames, spatial_weight, temporal_weight, cond_weight):
    clips, frames, rows, cols, chans = latents.shape
    slab = lax.axis_index("space")
    frame_ids = slab * frames + jnp.arange(frames, dtype=jnp.int32)
    mask = (frame_ids[None, :] < valid_frames[:, None]).astype(jnp.bfloat16)[:, :, None, None, None]
    mask_f = mask.astype(jnp.float32)
    masked = latents * mask
    first = from_root(masked[:, 0], "space", 0)
    rows_pad = own_window(lax.all_gather(masked, "tm", axis=2, tiled=True), rows)
    padded = jnp.pad(rows_pad, ((0, 0), (0, 0), (0, 0), (1, 1), (0, 0)))
    pre = spatial_sum(padded, spatial_weight, False)
    act = jax.nn.silu(pre).astype(jnp.bfloat16)
    cot = cotangent * mask
    earlier = shifted(act, "space", 1)
    act_pad = jnp.concatenate([earlier, act], axis=1)
    mixed = lag_forward(act_pad, temporal_weight, frames)
    later = shifted(cot, "space", -1)
    cot_pad = jnp.concatenate([cot, later], axis=1)
    dact = lag_backward(cot_pad, temporal_weight, frames)
    temporal_terms = lag_grads(act_pad, cot, frames)
    cond = jnp.dot(first, cond_weight, preferred_element_type=jnp.float32)
    output = ((masked.astype(jnp.float32) + mixed + cond[:, None]) * mask_f).astype(jnp.bfloat16)
    sig = jax.nn.sigmoid(pre)
    dpre = (dact * sig * (1.0 + pre * (1.0 - sig))).astype(jnp.bfloat16)
    cot_sum = lax.psum(jnp.sum(cot, axis=1, dtype=jnp.float32), "space")
    cond_back = jnp.dot(cot_sum, cond_weight.astype(jnp.float32).T, precision=lax.Precision.HIGHEST)
    dpre_rows = own_window(lax.all_gather(dpre, "tm", axis=2, tiled=True), rows)
    dpre_pad = jnp.pad(dpre_rows, ((0, 0), (0, 0), (0, 0), (1, 1), (0, 0)))
    dmasked = spatial_sum(dpre_pad, spatial_weight, True)
    is_first = (frame_ids == 0).astype(jnp.float32)[None, :, None, None, None]
    grad_latents = (
        (cot.astype(jnp.float32) + dmasked + is_first * cond_back[:, None]) * mask_f
    ).astype(jnp.bfloat16)
    dims = (((0, 1, 2, 3), (0, 1, 2, 3)), ((), ()))
    spatial_terms = []
    for row_off in range(3):
        for col_off in range(3):
            piece = padded[:, :, row_off : row_off + rows, col_off : col_off + cols]
            spatial_terms.append(
                lax.dot_general(piece, dpre, dims, preferred_element_type=jnp.float32)
            )
    spatial_terms = jnp.stack(spatial_terms)
    is_owner = (slab == 0).astype(jnp.float32)
    cond_terms = is_owner * lax.dot_general(
        first.astype(jnp.float32),
        cot_sum,
        (((0, 1, 2), (0, 1, 2)), ((), ())),
        precision=lax.Precision.HIGHEST,
    )
    summed = lax.psum((spatial_terms, temporal_terms, cond_terms), ("space", "tm"))
    scale = (clips * frames * rows * cols * lax.axis_size("space") * lax.axis_size("tm")) ** (-0.5)
    grad_spatial = (summed[0] * scale).astype(jnp.bfloat16)
    grad_temporal = (summed[1] * scale).astype(jnp.bfloat16)
    grad_cond = (summed[2] * scale).astype(jnp.bfloat16)
    return (output, grad_latents, grad_spatial, grad_temporal, grad_cond)


def solution(mesh):
    return jax.shard_map(
        on_device,
        mesh=mesh,
        in_specs=(
            P("groups", "space", "tm", None, None),
            P("groups", "space", "tm", None, None),
            P("groups"),
            P(),
            P(),
            P(),
        ),
        out_specs=(
            P("groups", "space", "tm", None, None),
            P("groups", "space", "tm", None, None),
            P("groups", None, None),
            P("groups", None, None),
            P("groups", None),
        ),
        check_vma=False,
    )
```

profile of v0, /device:TPU:0, one launch (start us, length us, event | category | flops | bytes accessed | tf_op | source)
XLA Modules:
  0.0 338.7 jit_solution(10557166967447815481)
XLA Ops:
  8.8 1.4 broadcast_multiply_fusion.1
  11.2 2.7 convert_reduce_fusion
  14.5 1.3 collective-permute-start.1
  15.9 1.8 fusion.75
  17.7 75.7 %all-reduce.9.cloned.1.call-done = bf16[2,2,256,256]{3,2,1,0:T(8,128)(2,1)} async-done(((bf16[2,2,256,256]{3,2,1,0:T(8,128)(2,1)}), bf16[2,2,256,256]{3,2,1,0:T(8,128)(2,1)}) %all-reduce.9.cloned.1.call-update) | async-done | bytes 524304 | tf_op jit(solution)/shard_map/psum | solution.py:9
  93.3 2.3 fusion.47
  95.7 79.6 %all-reduce.11.cloned.1.call-done = f32[2,2,256,256]{3,2,1,0:T(8,128)} async-done(((f32[2,2,256,256]{3,2,1,0:T(8,128)}), f32[2,2,256,256]{3,2,1,0:T(8,128)}) %all-reduce.11.cloned.1.call-update) | async-done | bytes 1048592 | tf_op jit(solution)/shard_map/psum | solution.py:101
  175.3 3.0 fusion.13
  178.2 1.6 fusion.45
  179.9 1.8 fusion.3
  181.7 1.8 pad_dynamic-slice_fusion.1
  187.1 2.1 multiply_convert_fusion.3
  189.9 2.0 multiply_convert_fusion.1
  191.9 1.2 fusion.19
  193.2 3.5 %collective-permute-start = (bf16[2,2,2,256,256]{4,3,2,1,0:T(8,128)(2,1)}, bf16[2,2,2,256,256]{4,3,2,1,0:T(8,128)(2,1)S(1)}, u32[]{:S(2)}, u32[]{:S(2)}) collective-permute-start(bf16[2,2,2,256,256]{4,3,2,1,0:T(8,128)(2,1)} %get-tuple-element.12), channel_id=1, source_target_pairs={{0,2},{2,4},{4,6},{6,8},{8,10},{10,12},{12,14},{1,3},{3,5},{5,7},{... | collective-permute-start | bytes 3145736 | tf_op jit(solution)/shard_map/ppermute | solution.py:15
  196.7 2.4 fusion.12
  199.1 1.2 fusion.18
  200.3 1.2 fusion.17
  201.5 1.2 fusion.11
  202.7 1.2 fusion.16
  203.8 1.2 fusion.15
  205.9 1.2 fusion.10
  207.1 1.2 fusion.14
  208.3 2.7 fusion.77
  211.0 7.8 %collective-permute-done = bf16[2,2,2,256,256]{4,3,2,1,0:T(8,128)(2,1)S(1)} collective-permute-done((bf16[2,2,2,256,256]{4,3,2,1,0:T(8,128)(2,1)}, bf16[2,2,2,256,256]{4,3,2,1,0:T(8,128)(2,1)S(1)}, u32[]{:S(2)}, u32[]{:S(2)}) %collective-permute-start) | collective-permute-done | bytes 1048608 | tf_op jit(solution)/shard_map/ppermute | solution.py:15
  219.8 1.0 pad_maximum_fusion.5
  220.8 1.2 copy-done.8
  224.6 1.7 multiply_convert_fusion.2
  226.3 1.8 pad_dynamic-slice_fusion
  233.1 2.2 fusion.2
  235.3 91.7 %all-reduce.13.cloned.1.call-done = (f32[9,256,256]{2,1,0:T(8,128)}, f32[3,256,256]{2,1,0:T(8,128)}, f32[256,256]{1,0:T(8,128)}) async-done(((f32[9,256,256]{2,1,0:T(8,128)}, f32[3,256,256]{2,1,0:T(8,128)}, f32[256,256]{1,0:T(8,128)}), (f32[9,256,256]{2,1,0:T(8,128)}, f32[3,256,256]{2,1,0:T(8,128)}, f32[256,256]{1,0:T(8,128)})) %all-reduce.13.cloned.1.call-update) | async-done | bytes 3407888 | tf_op jit(solution)/shard_map/psum | solution.py:126
  327.0 3.0 multiply_convert_fusion
  (92 shorter events, 17.6 us)
Async XLA Ops:
  8.0 85.3 %copy-start = (bf16[256,256]{1,0:T(8,128)(2,1)S(1)}, bf16[256,256]{1,0:T(8,128)(2,1)}, u32[]{:S(2)}) copy-start(bf16[256,256]{1,0:T(8,128)(2,1)} %param.11) | copy-start | bytes 393220
  8.0 85.3 %all-reduce.9.cloned.1.call-start = ((), (), s32[]{:S(2)}) async-start(), calls=%async_computation.1 | async-start | bytes 1048576 | tf_op jit(solution)/shard_map/psum | solution.py:9
  10.2 3.7 %copy-start.11 = (bf16[2,2,2,256,256]{4,3,2,1,0:T(8,128)(2,1)}, bf16[2,2,2,256,256]{4,3,2,1,0:T(8,128)(2,1)S(1)}, u32[]{:S(2)}) copy-start(bf16[2,2,2,256,256]{4,3,2,1,0:T(8,128)(2,1)S(1)} %broadcast_multiply_fusion.1) | copy-start | bytes 3145732
  11.1 4.8 %copy-start.21 = (bf16[3,256,256]{2,1,0:T(8,128)(2,1)S(1)}, bf16[3,256,256]{2,1,0:T(8,128)(2,1)}, u32[]{:S(2)}) copy-start(bf16[3,256,256]{2,1,0:T(8,128)(2,1)} %param.10) | copy-start | bytes 1179652
  11.1 164.2 %all-reduce.11.cloned.1.call-start = ((), (), s32[]{:S(2)}) async-start(), calls=%async_computation.3 | async-start | bytes 2097152 | tf_op jit(solution)/shard_map/psum | solution.py:101
  13.9 166.0 %copy-start.4 = (bf16[2,2,2,256,256]{4,3,2,1,0:T(8,128)(2,1)}, bf16[2,2,2,256,256]{4,3,2,1,0:T(8,128)(2,1)S(1)}, u32[]{:S(2)}) copy-start(bf16[2,2,2,256,256]{4,3,2,1,0:T(8,128)(2,1)S(1)} %get-tuple-element.9) | copy-start | bytes 3145732
  13.9 167.8 %all-gather.3.cloned.1.call-start = ((), (), s32[]{:S(2)}) async-start(), calls=%async_computation | async-start | bytes 3145728 | tf_op jit(solution)/shard_map/all_gather | solution.py:85
  14.5 211.8 %all-gather.5.cloned.1.call-start = ((), (), s32[]{:S(2)}) async-start(), calls=%async_computation.2 | async-start | bytes 3145728 | tf_op jit(solution)/shard_map/all_gather | solution.py:103
  14.5 165.3 %collective-permute-start.1 = (bf16[2,2,2,256,256]{4,3,2,1,0:T(8,128)(2,1)S(1)}, bf16[2,2,2,256,256]{4,3,2,1,0:T(8,128)(2,1)S(1)}, u32[]{:S(2)}, u32[]{:S(2)}) collective-permute-start(bf16[2,2,2,256,256]{4,3,2,1,0:T(8,128)(2,1)S(1)} %get-tuple-element.9), channel_id=1, source_target_pairs={{2,0},{4,2},{6,4},{8,6},{10,8},{12,10},{14,12},{3,1},{5,3},{7,5},{... | collective-permute-start | bytes 3145736 | tf_op jit(solution)/shard_map/ppermute | solution.py:15
  175.3 3.0 copy-start.18
  179.8 1.8 copy-start.23
  181.7 1.8 copy-start.14
  187.1 2.2 copy-start.19
  187.1 2.3 copy-start.20
  187.1 2.8 copy-start.24
  193.1 6.0 %copy-start.3 = (bf16[2,2,2,256,256]{4,3,2,1,0:T(8,128)(2,1)S(1)}, bf16[2,2,2,256,256]{4,3,2,1,0:T(8,128)(2,1)}, u32[]{:S(2)}) copy-start(bf16[2,2,2,256,256]{4,3,2,1,0:T(8,128)(2,1)} %copy-done.2) | copy-start | bytes 3145732
  193.2 133.8 %all-reduce.13.cloned.1.call-start = ((), (), s32[]{:S(2)}) async-start(), calls=%async_computation.4 | async-start | bytes 6815744 | tf_op jit(solution)/shard_map/psum | solution.py:126
  193.2 25.7 %collective-permute-start = (bf16[2,2,2,256,256]{4,3,2,1,0:T(8,128)(2,1)}, bf16[2,2,2,256,256]{4,3,2,1,0:T(8,128)(2,1)S(1)}, u32[]{:S(2)}, u32[]{:S(2)}) collective-permute-start(bf16[2,2,2,256,256]{4,3,2,1,0:T(8,128)(2,1)} %get-tuple-element.12), channel_id=1, source_target_pairs={{0,2},{2,4},{4,6},{6,8},{8,10},{10,12},{12,14},{1,3},{3,5},{5,7},{... | collective-permute-start | bytes 3145736 | tf_op jit(solution)/shard_map/ppermute | solution.py:15
  203.8 1.2 copy-start.5
  203.8 1.6 copy-start.7
  220.8 1.2 copy-start.8
  220.8 1.5 copy-start.10
  220.8 1.6 copy-start.22
  222.4 1.2 copy-start.12
  222.4 1.9 copy-start.13
  222.4 2.2 copy-start.17
  226.3 1.9 copy-start.15
  231.6 1.2 copy-start.6
  231.6 1.6 copy-start.16
  327.0 3.0 copy-start.25
  327.0 4.5 %copy-start.1 = (bf16[256,256]{1,0:T(8,128)(2,1)S(1)}, bf16[256,256]{1,0:T(8,128)(2,1)}, u32[]{:S(2)}) copy-start(bf16[256,256]{1,0:T(8,128)(2,1)} %param.11) | copy-start | bytes 393220
  327.0 3.9 %copy-start.26 = (f32[256,256]{1,0:T(8,128)S(1)}, f32[256,256]{1,0:T(8,128)}, u32[]{:S(2)}) copy-start(f32[256,256]{1,0:T(8,128)} %get-tuple-element.7) | copy-start | bytes 786436
  (2 other events, 2.2 us)
Sparse Core Ops, SparseCore 0:
  12.8 80.4 all-reduce.8
  97.8 77.4 all-reduce.10
  220.9 105.9 all-reduce.12
Sparse Core Ops, SparseCore 1:
  16.5 13.1 all-gather.2
  193.2 10.0 all-gather.4
where the time goes:
time: 339 us
  waiting for transfers between devices  255 us (75%)
  matrix products  42.3 us (12%)
  between operations  15.5 us (5%)
  other arithmetic  11.2 us (3%)
  local copies, waits for them, and re-layouts  9.27 us (3%)
  starting transfers between devices  5.03 us (1%)
    psum x1, waiting for transfers between devices, on_device(): lax.psum((spatial_terms, temporal_terms, cond_terms), ('space', 'tm'))  91.7 us
    psum x1, waiting for transfers between devices, on_device(): cot_sum = lax.psum(jnp.sum(cot, axis=1, dtype=jnp.float32), 'space')  79.6 us
    psum x1, waiting for transfers between devices, from_root(): return lax.psum(block, axis)  75.7 us
    dot_general x9, matrix products, on_device(): lax.dot_general(piece, dpre, dims, preferred_element_type=jnp.float32)  11.9 us
    dot_general x18, matrix products, spatial_sum(): total = total + jnp.dot(piece, kernel, preferred_element_type=jnp.float32)  11.7 us
    ppermute x2, waiting for transfers between devices, shifted(): return lax.ppermute(value, axis, pairs)  7.84 us
  transfers between devices with their start and end apart: 7, of which 4 were waited for; matrix products, arithmetic and copies ran while one was open for 12% of the time, Pallas kernels for 0%

commit v1 on v0

v1 whole, which is shorter than its diff:
```python
import jax
import jax.numpy as jnp
from jax import lax
from jax.sharding import PartitionSpec as P


def broadcast_first(value, axis):
    count = lax.axis_size(axis)
    me = lax.axis_index(axis)
    step = 1
    while step < count:
        pairs = [(i, i + step) for i in range(step) if i + step < count]
        got = lax.ppermute(value, axis, pairs)
        value = jnp.where((me >= step) & (me < 2 * step), got, value)
        step *= 2
    return value


def reduce_first(value, axis):
    count = lax.axis_size(axis)
    step = 1
    while step < count:
        step *= 2
    step //= 2
    while step >= 1:
        pairs = [(i + step, i) for i in range(step) if i + step < count]
        got = lax.ppermute(value.astype(jnp.bfloat16), axis, pairs)
        value = value + got.astype(jnp.float32)
        step //= 2
    return value


def swap(value, axis, bit):
    count = lax.axis_size(axis)
    return lax.ppermute(value, axis, [(i, i ^ bit) for i in range(count)])


def sum_all(value, order):
    sides = []
    for axis, bit in order:
        side = (lax.axis_index(axis) // bit) % 2
        half = value.shape[0] // 2
        low, high = value[:half], value[half:]
        mine = jnp.where(side == 0, low, high)
        other = jnp.where(side == 0, high, low).astype(jnp.bfloat16)
        value = mine + swap(other, axis, bit).astype(jnp.float32)
        sides.append(side)
    value = value.astype(jnp.bfloat16)
    for (axis, bit), side in zip(reversed(order), reversed(sides)):
        got = swap(value, axis, bit)
        value = jnp.where(
            side == 0,
            jnp.concatenate([value, got], axis=0),
            jnp.concatenate([got, value], axis=0),
        )
    return value


def shifted(value, axis, by):
    count = lax.axis_size(axis)
    pairs = [(i, i + by) for i in range(count) if 0 <= i + by < count]
    return lax.ppermute(value, axis, pairs)


def spatial_sum(padded, weights, flip):
    rows = padded.shape[2] - 2
    cols = padded.shape[3] - 2
    total = jnp.zeros(padded.shape[:2] + (rows, cols, weights.shape[2]), jnp.float32)
    for row_off in range(3):
        for col_off in range(3):
            if flip:
                piece = padded[
                    :, :, 2 - row_off : 2 - row_off + rows, 2 - col_off : 2 - col_off + cols
                ]
                kernel = weights[3 * row_off + col_off].T
            else:
                piece = padded[:, :, row_off : row_off + rows, col_off : col_off + cols]
                kernel = weights[3 * row_off + col_off]
            total = total + jnp.dot(piece, kernel, preferred_element_type=jnp.float32)
    return total


def lag_forward(padded_act, weights, count):
    total = 0.0
    for lag in range(3):
        total = total + jnp.dot(
            padded_act[:, 2 - lag : 2 - lag + count],
            weights[lag],
            preferred_element_type=jnp.float32,
        )
    return total


def lag_backward(padded_cot, weights, count):
    total = 0.0
    for lag in range(3):
        total = total + jnp.dot(
            padded_cot[:, lag : lag + count], weights[lag].T, preferred_element_type=jnp.float32
        )
    return total


DIMS = (((0, 1, 2, 3), (0, 1, 2, 3)), ((), ()))


def outer(left, right):
    return lax.dot_general(left, right, DIMS, preferred_element_type=jnp.float32)


def with_halo(value):
    low = shifted(value[:, :, -1:], "tm", 1)
    high = shifted(value[:, :, :1], "tm", -1)
    rows = jnp.concatenate([low, value, high], axis=2)
    return jnp.pad(rows, ((0, 0), (0, 0), (0, 0), (1, 1), (0, 0)))


def on_device(latents, cotangent, valid_frames, spatial_weight, temporal_weight, cond_weight):
    clips, frames, rows, cols, chans = latents.shape
    slab = lax.axis_index("space")
    frame_ids = slab * frames + jnp.arange(frames, dtype=jnp.int32)
    mask = (frame_ids[None, :] < valid_frames[:, None]).astype(jnp.bfloat16)[:, :, None, None, None]
    mask_f = mask.astype(jnp.float32)
    masked = latents * mask
    cot = cotangent * mask
    padded = with_halo(masked)
    later = shifted(cot, "space", -1)
    first = broadcast_first(masked[:, 0], "space")
    cot_sum = reduce_first(jnp.sum(cot, axis=1, dtype=jnp.float32), "space")
    pre = spatial_sum(padded, spatial_weight, False)
    act = jax.nn.silu(pre).astype(jnp.bfloat16)
    earlier = shifted(act, "space", 1)
    cot_pad = jnp.concatenate([cot, later], axis=1)
    dact = lag_backward(cot_pad, temporal_weight, frames)
    sig = jax.nn.sigmoid(pre)
    dpre = (dact * sig * (1.0 + pre * (1.0 - sig))).astype(jnp.bfloat16)
    dpre_pad = with_halo(dpre)
    terms = []
    for row_off in range(3):
        for col_off in range(3):
            piece = padded[:, :, row_off : row_off + rows, col_off : col_off + cols]
            terms.append(outer(piece, dpre))
    for lag in range(3):
        terms.append(outer(act, cot_pad[:, lag : lag + frames]))
    wide_first = jnp.broadcast_to(first[:, None], cot.shape)
    terms.append(outer(wide_first, cot))
    space = lax.axis_size("space")
    bits = [1 << k for k in range(1, space.bit_length() - 1)]
    order = [("tm", 1)] + [("space", bit) for bit in bits] + [("space", 1)]
    grads = sum_all(jnp.concatenate(terms, axis=0), order)
    dmasked = spatial_sum(dpre_pad, spatial_weight, True)
    cond_back = jnp.dot(cot_sum, cond_weight.astype(jnp.float32).T, precision=lax.Precision.HIGHEST)
    is_first = (frame_ids == 0).astype(jnp.float32)[None, :, None, None, None]
    grad_latents = (
        (cot.astype(jnp.float32) + dmasked + is_first * cond_back[:, None]) * mask_f
    ).astype(jnp.bfloat16)
    act_pad = jnp.concatenate([earlier, act], axis=1)
    mixed = lag_forward(act_pad, temporal_weight, frames)
    cond = jnp.dot(first, cond_weight, preferred_element_type=jnp.float32)
    output = ((masked.astype(jnp.float32) + mixed + cond[:, None]) * mask_f).astype(jnp.bfloat16)
    scale = (clips * frames * rows * cols * lax.axis_size("space") * lax.axis_size("tm")) ** (-0.5)
    scaled = (grads.astype(jnp.float32) * scale).astype(jnp.bfloat16)
    scaled = scaled.reshape(13, chans, chans)
    return (output, grad_latents, scaled[:9], scaled[9:12], scaled[12])


def solution(mesh):
    return jax.shard_map(
        on_device,
        mesh=mesh,
        in_specs=(
            P("groups", "space", "tm", None, None),
            P("groups", "space", "tm", None, None),
            P("groups"),
            P(),
            P(),
            P(),
        ),
        out_specs=(
            P("groups", "space", "tm", None, None),
            P("groups", "space", "tm", None, None),
            P("groups", None, None),
            P("groups", None, None),
            P("groups", None),
        ),
        check_vma=False,
    )
```

time: 339 us -> 189 us (0.56)
  waiting for transfers between devices: 255 us -> 68.5 us
  starting transfers between devices: 5.03 us -> 42 us
  between operations: 15.5 us -> 1.3 us
  matrix products: 42.3 us -> 51.1 us
  other arithmetic: 11.2 us -> 17 us
    psum x3 -> x0, waiting for transfers between devices: 247 us -> none  [the longest x1 91.7 us: on_device(): lax.psum((spatial_terms, temporal_terms, cond_terms), ('space', 'tm'))]
    ppermute x0 -> x14, waiting for transfers between devices: none -> 68.4 us  [the longest x8 33.7 us: swap(): return lax.ppermute(value, axis, [(i, i ^ bit) for i in range(count)])]
    ppermute x0 -> x14, starting transfers between devices: none -> 28 us  [the longest x8 15.9 us: swap(): return lax.ppermute(value, axis, [(i, i ^ bit) for i in range(count)])]
    ppermute x2 -> x6, starting transfers between devices: 4.83 us -> 14 us  [shifted(): return lax.ppermute(value, axis, pairs)]
    ppermute x2 -> x6, waiting for transfers between devices: 7.84 us -> 0.02 us  [shifted(): return lax.ppermute(value, axis, pairs)]
    dot_general x18, matrix products: 11.7 us -> 18.2 us  [spatial_sum(): total = total + jnp.dot(piece, kernel, preferred_element_type=jnp.float32)]
    unnamed x54 -> x32, local copies, waits for them, and re-layouts: 5.67 us -> 0.08 us
    slice x0 -> x5, local copies, waits for them, and re-layouts: none -> 4.59 us  [the longest x3 2.52 us: on_device(): return (output, grad_latents, scaled[:9], scaled[9:12], scaled[12])]
  transfers between devices with their start and end apart: 7 -> 20, of which waited for: 4 -> 9; matrix products, arithmetic and copies ran while one was open for 12% -> 37% of each run, Pallas kernels for 0% -> 0%
where the time goes in v1:
time: 189 us; the launch traced here: 187 us
  waiting for transfers between devices  68.5 us (36%)
  matrix products  51.1 us (27%)
  starting transfers between devices  42 us (22%)
  other arithmetic  17 us (9%)
  local copies, waits for them, and re-layouts  7.54 us (4%)
    ppermute x8, waiting for transfers between devices, swap(): return lax.ppermute(value, axis, [(i, i ^ bit) for i in range(count)])  33.7 us
    ppermute x3, waiting for transfers between devices, broadcast_first(): got = lax.ppermute(value, axis, pairs)  24.5 us
    dot_general x13, matrix products, outer(): lax.dot_general(left, right, DIMS, preferred_element_type=jnp.float32)  18.6 us
    dot_general x18, matrix products, spatial_sum(): total = total + jnp.dot(piece, kernel, preferred_element_type=jnp.float32)  18.2 us
    ppermute x8, starting transfers between devices, swap(): return lax.ppermute(value, axis, [(i, i ^ bit) for i in range(count)])  15.9 us
    ppermute x6, starting transfers between devices, shifted(): return lax.ppermute(value, axis, pairs)  14 us
    ppermute x3, waiting for transfers between devices, reduce_first(): got = lax.ppermute(value.astype(jnp.bfloat16), axis, pairs)  10.2 us
    ppermute x3, starting transfers between devices, broadcast_first(): got = lax.ppermute(value, axis, pairs)  8.31 us
  transfers between devices with their start and end apart: 20, of which 9 were waited for; matrix products, arithmetic and copies ran while one was open for 37% of the time, Pallas kernels for 0%

profile of v1, /device:TPU:0, one launch (start us, length us, event | category | flops | bytes accessed | tf_op | source)
XLA Modules:
  0.0 187.4 jit_solution(11075313650007865224)
XLA Ops:
  3.9 3.2 %collective-permute-start = (bf16[2,2,1,256,256]{4,3,2,1,0:T(8,128)(2,1)}, bf16[2,2,1,256,256]{4,3,2,1,0:T(8,128)(2,1)}, u32[]{:S(2)}, u32[]{:S(2)}) collective-permute-start(bf16[2,2,1,256,256]{4,3,2,1,0:T(8,128)(2,1)} %get-tuple-element.11), channel_id=1, source_target_pairs={{0,1},{2,3},{4,5},{6,7},{8,9},{10,11},{12,13},{14,15},{16,17},{18,... | collective-permute-start | bytes 1572872 | tf_op jit(solution)/shard_map/ppermute | solution.py:62
  10.9 5.7 %collective-permute-start.3 = (bf16[2,2,256,256]{3,2,1,0:T(8,128)(2,1)}, bf16[2,2,256,256]{3,2,1,0:T(8,128)(2,1)}, u32[]{:S(2)}, u32[]{:S(2)}) collective-permute-start(bf16[2,2,256,256]{3,2,1,0:T(8,128)(2,1)} %slice_bitcast_fusion), channel_id=1, source_target_pairs={{0,2},{1,3},{16,18},{17,19}} | collective-permute-start | bytes 1572872 | tf_op jit(solution)/shard_map/ppermute | solution.py:13
  20.8 2.1 %select_maximum_fusion.2 = bf16[2,2,4,258,256]{4,3,2,1,0:T(8,128)(2,1)S(1)} fusion(bf16[2,2,1,256,256]{4,3,2,1,0:T(8,128)(2,1)} %collective-permute-done.1, bf16[2,2,2,256,256]{4,3,2,1,0:T(8,128)(2,1)S(1)} %broadcast_multiply_fusion.1, bf16[2,2,1,256,256]{4,3,2,1,0:T(8,128)(2,1)} %collective-permute-done), kind=kLoop, calls=%fused_computation.8 | loop fusion | flops 12681216 | bytes 4210688 | tf_op jit(solution)/shard_map/concatenate | solution.py:113
  24.2 24.5 %collective-permute-done.3 = bf16[2,2,256,256]{3,2,1,0:T(8,128)(2,1)} collective-permute-done((bf16[2,2,256,256]{3,2,1,0:T(8,128)(2,1)}, bf16[2,2,256,256]{3,2,1,0:T(8,128)(2,1)}, u32[]{:S(2)}, u32[]{:S(2)}) %collective-permute-start.3) | collective-permute-done | bytes 524320 | tf_op jit(solution)/shard_map/ppermute | solution.py:13
  51.0 10.2 %collective-permute-done.9 = bf16[2,2,256,256]{3,2,1,0:T(8,128)(2,1)} collective-permute-done((bf16[2,2,256,256]{3,2,1,0:T(8,128)(2,1)}, bf16[2,2,256,256]{3,2,1,0:T(8,128)(2,1)}, u32[]{:S(2)}, u32[]{:S(2)}) %collective-permute-start.9) | collective-permute-done | bytes 524320 | tf_op jit(solution)/shard_map/ppermute | solution.py:27
  66.6 2.3 %multiply_convert_fusion.3 = (bf16[2,2,2,256,256]{4,3,2,1,0:T(8,128)(2,1)}, f32[2,2,2,256,256]{4,3,2,1,0:T(8,128)S(1)}) fusion(bf16[9,256,256]{2,1,0:T(8,128)(2,1)S(1)} %copy-done.9, bf16[2,2,4,258,256]{4,3,2,1,0:T(8,128)(2,1)S(1)} %select_maximum_fusion.2, f32[2,2,2,256,256]{4,3,2,1,0:T(8,128)S(1)} %fusion.51, f32[2,2,2,256,256]{4,3,2,1,0:T(8,128)S(1)} %fusion.59, ...), kind=kOutput, calls=%fused_computation.24 | convolution fusion | flops 275251200 | bytes 21102592 | tf_op jit(solution)/shard_map/dot_general | solution.py:79
  68.9 2.3 %collective-permute-start.2 = (bf16[2,2,2,256,256]{4,3,2,1,0:T(8,128)(2,1)}, bf16[2,2,2,256,256]{4,3,2,1,0:T(8,128)(2,1)}, u32[]{:S(2)}, u32[]{:S(2)}) collective-permute-start(bf16[2,2,2,256,256]{4,3,2,1,0:T(8,128)(2,1)} %get-tuple-element.15), channel_id=1, source_target_pairs={{0,2},{2,4},{4,6},{6,8},{8,10},{10,12},{12,14},{1,3},{3,5},{5,7},{... | collective-permute-start | bytes 3145736 | tf_op jit(solution)/shard_map/ppermute | solution.py:62
  71.2 3.0 %fusion.112 = f32[2,2,2,256,256]{4,3,2,1,0:T(8,128)} fusion(bf16[2,2,2,256,256]{4,3,2,1,0:T(8,128)(2,1)} %get-tuple-element.15, bf16[3,256,256]{2,1,0:T(8,128)(2,1)S(1)} %copy-done.13), kind=kOutput, calls=%fused_computation.153 | convolution fusion | flops 268435456 | bytes 3276800 | tf_op jit(solution)/shard_map/dot_general | solution.py:86
  75.7 2.3 %multiply_convert_fusion.1 = bf16[2,2,2,256,256]{4,3,2,1,0:T(8,128)(2,1)S(1)} fusion(f32[2,2,2,256,256]{4,3,2,1,0:T(8,128)S(1)} %get-tuple-element.16, f32[2,2,2,256,256]{4,3,2,1,0:T(8,128)S(1)} %fusion.110, f32[2,2,2,256,256]{4,3,2,1,0:T(8,128)S(1)} %fusion.9, bf16[2,2,2,256,256]{4,3,2,1,0:T(8,128)(2,1)} %collective-permute-done.6, ...), kind=kOutput, calls=%fused_computation.22 | convolution fusion | flops 274202624 | bytes 8519680 | tf_op jit(solution)/shard_map/dot_general | solution.py:97
  87.0 4.6 %collective-permute-start.7 = (bf16[2,2,1,256,256]{4,3,2,1,0:T(8,128)(2,1)}, bf16[2,2,1,256,256]{4,3,2,1,0:T(8,128)(2,1)}, u32[]{:S(2)}, u32[]{:S(2)}) collective-permute-start(bf16[2,2,1,256,256]{4,3,2,1,0:T(8,128)(2,1)} %get-tuple-element.10), channel_id=1, source_target_pairs={{0,1},{2,3},{4,5},{6,7},{8,9},{10,11},{12,13},{14,15},{16,17},{18,... | collective-permute-start | bytes 1572872 | tf_op jit(solution)/shard_map/ppermute | solution.py:62
  91.6 2.2 %fusion.21 = f32[1792,256]{1,0:T(8,128)} fusion(f32[1792,256]{1,0:T(8,128)} %get-tuple-element.14, bf16[2,2,2,256,256]{4,3,2,1,0:T(8,128)(2,1)S(1)} %multiply_convert_fusion.1, bf16[2,2,1,256,256]{4,3,2,1,0:T(8,128)(2,1)} %collective-permute-done.1, bf16[2,2,2,256,256]{4,3,2,1,0:T(8,128)(2,1)S(1)} %broadcast_multiply_fusion.1), kind=kOutput, calls=%fused_computation.41 | convolution fusion | flops 271581184 | bytes 2883584 | tf_op jit(solution)/shard_map/dot_general | solution.py:107
  95.0 2.4 %fusion.26 = f32[1792,256]{1,0:T(8,128)} fusion(f32[1792,256]{1,0:T(8,128)} %fusion.27, bf16[2,2,2,256,256]{4,3,2,1,0:T(8,128)(2,1)} %get-tuple-element.15, bf16[2,2,2,256,256]{4,3,2,1,0:T(8,128)(2,1)S(1)} %get-tuple-element.6), kind=kOutput, calls=%fused_computation.51 | convolution fusion | flops 268435456 | bytes 2359296 | tf_op jit(solution)/shard_map/dot_general | solution.py:107
  97.4 2.3 %fusion.75 = bf16[2,2,256,256]{3,2,1,0:T(8,128)(2,1)} fusion(bf16[2,2,256,256]{3,2,1,0:T(8,128)(2,1)S(1)} %collective-permute-done.10, f32[2,2,256,256]{3,2,1,0:T(8,128)S(1)} %copy-done.2, bf16[2,2,256,256]{3,2,1,0:T(8,128)(2,1)} %collective-permute-done.9), kind=kLoop, calls=%fused_computation.119 | loop fusion | flops 1310720 | bytes 2621440 | tf_op jit(solution)/shard_map/convert_element_type | solution.py:27
  101.0 2.5 %fusion.25 = f32[1792,256]{1,0:T(8,128)} fusion(f32[1792,256]{1,0:T(8,128)} %fusion.26, bf16[2,2,2,256,256]{4,3,2,1,0:T(8,128)(2,1)} %get-tuple-element.15, bf16[2,2,2,256,256]{4,3,2,1,0:T(8,128)(2,1)} %collective-permute-done.6, bf16[2,2,2,256,256]{4,3,2,1,0:T(8,128)(2,1)S(1)} %get-tuple-element.6), kind=kOutput, calls=%fused_computation.49 | convolution fusion | flops 268959744 | bytes 3407872 | tf_op jit(solution)/shard_map/dot_general | solution.py:107
  103.5 2.7 %fusion.24 = f32[1792,256]{1,0:T(8,128)} fusion(f32[1792,256]{1,0:T(8,128)} %fusion.25, bf16[2,2,2,256,256]{4,3,2,1,0:T(8,128)(2,1)} %get-tuple-element.15, bf16[2,2,2,256,256]{4,3,2,1,0:T(8,128)(2,1)} %collective-permute-done.6), kind=kOutput, calls=%fused_computation.47 | convolution fusion | flops 268435456 | bytes 2359296 | tf_op jit(solution)/shard_map/dot_general | solution.py:107
  106.2 1.8 fusion.91
  108.9 2.0 %copy.23 = bf16[2,2,256,256]{2,3,1,0:T(8,128)(2,1)} copy(bf16[2,2,256,256]{3,2,1,0:T(8,128)(2,1)} %broadcast_select_fusion.2) | data formatting | bytes 1048576 | tf_op jit(solution)/shard_map/jit(_where)/select_n | solution.py:14
  110.9 2.4 %fusion.23 = f32[1792,256]{1,0:T(8,128)} fusion(f32[1792,256]{1,0:T(8,128)} %fusion.24, bf16[2,2,2,256,256]{4,3,2,1,0:T(8,128)(2,1)S(1)} %get-tuple-element.6, bf16[2,2,256,256]{2,3,1,0:T(8,128)(2,1)} %copy.23), kind=kOutput, calls=%fused_computation.45 | convolution fusion | flops 268435456 | bytes 1835008 | tf_op jit(solution)/shard_map/dot_general | solution.py:107
  113.3 1.7 select_convert_fusion
  115.1 2.1 %select_maximum_fusion = bf16[2,2,4,258,256]{4,3,2,1,0:T(8,128)(2,1)S(1)} fusion(bf16[2,2,1,256,256]{4,3,2,1,0:T(8,128)(2,1)} %collective-permute-done.8, bf16[2,2,2,256,256]{4,3,2,1,0:T(8,128)(2,1)S(1)} %multiply_convert_fusion.1, bf16[2,2,1,256,256]{4,3,2,1,0:T(8,128)(2,1)} %collective-permute-done.7), kind=kLoop, calls=%fused_computation.6 | loop fusion | flops 12681216 | bytes 4210688 | tf_op jit(solution)/shard_map/concatenate | solution.py:113
  119.2 1.7 convert_add_fusion.1
  121.0 2.8 %collective-permute-start.13 = (bf16[832,256]{1,0:T(8,128)(2,1)S(1)}, bf16[832,256]{1,0:T(8,128)(2,1)S(1)}, u32[]{:S(2)}, u32[]{:S(2)}) collective-permute-start(bf16[832,256]{1,0:T(8,128)(2,1)S(1)} %select_convert_fusion.1), channel_id=1, source_target_pairs={{0,4},{2,6},{4,0},{6,2},{8,12},{10,14},{12,8},{14,10},{1,5},{3,7},... | collective-permute-start | bytes 1277960 | tf_op jit(solution)/shard_map/ppermute | solution.py:35
  124.3 2.0 %fusion.48 = f32[2,2,256,256]{3,2,1,0:T(8,128)S(1)} fusion(bf16[2,2,256,256]{3,2,1,0:T(8,128)(2,1)} %collective-permute-done.11, bf16[2,2,256,256]{3,2,1,0:T(8,128)(2,1)S(1)} %copy-done.12, f32[2,2,256,256]{3,2,1,0:T(8,128)S(1)} %copy-done.3, bf16[2,2,256,256]{3,2,1,0:T(8,128)(2,1)} %collective-permute-done.9, bf16[256,256]{1,0:T(8,128)(2,1)S(1)} %copy-done), kind=kOutput, calls=%fused_computation.80 | convolution fusion | flops 806879232 | bytes 3801088 | tf_op jit(solution)/shard_map/dot_general | solution.py:151
  126.3 7.8 %collective-permute-done.13 = bf16[832,256]{1,0:T(8,128)(2,1)S(1)} collective-permute-done((bf16[832,256]{1,0:T(8,128)(2,1)S(1)}, bf16[832,256]{1,0:T(8,128)(2,1)S(1)}, u32[]{:S(2)}, u32[]{:S(2)}) %collective-permute-start.13) | collective-permute-done | bytes 426016 | tf_op jit(solution)/shard_map/ppermute | solution.py:35
  134.3 3.4 %collective-permute-start.14 = (bf16[416,256]{1,0:T(8,128)(2,1)S(1)}, bf16[416,256]{1,0:T(8,128)(2,1)S(1)}, u32[]{:S(2)}, u32[]{:S(2)}) collective-permute-start(bf16[416,256]{1,0:T(8,128)(2,1)S(1)} %select_convert_fusion.2), channel_id=1, source_target_pairs={{0,8},{2,10},{4,12},{6,14},{8,0},{10,2},{12,4},{14,6},{1,9},{3,11}... | collective-permute-start | bytes 638984 | tf_op jit(solution)/shard_map/ppermute | solution.py:35
  139.2 8.3 %collective-permute-done.14 = bf16[416,256]{1,0:T(8,128)(2,1)S(1)} collective-permute-done((bf16[416,256]{1,0:T(8,128)(2,1)S(1)}, bf16[416,256]{1,0:T(8,128)(2,1)S(1)}, u32[]{:S(2)}, u32[]{:S(2)}) %collective-permute-start.14) | collective-permute-done | bytes 213024 | tf_op jit(solution)/shard_map/ppermute | solution.py:35
  147.6 7.3 %collective-permute-start.15 = (bf16[208,256]{1,0:T(8,128)(2,1)S(1)}, bf16[208,256]{1,0:T(8,128)(2,1)S(1)}, u32[]{:S(2)}, u32[]{:S(2)}) collective-permute-start(bf16[208,256]{1,0:T(8,128)(2,1)S(1)} %select_convert_fusion.3), channel_id=1, source_target_pairs={{0,2},{2,0},{4,6},{6,4},{8,10},{10,8},{12,14},{14,12},{1,3},{3,1},... | collective-permute-start | bytes 319496 | tf_op jit(solution)/shard_map/ppermute | solution.py:35
  157.7 2.1 %collective-permute-start.16 = (bf16[208,256]{1,0:T(8,128)(2,1)S(1)}, bf16[208,256]{1,0:T(8,128)(2,1)S(1)}, u32[]{:S(2)}, u32[]{:S(2)}) collective-permute-start(bf16[208,256]{1,0:T(8,128)(2,1)S(1)} %add_convert_fusion), channel_id=1, source_target_pairs={{0,2},{2,0},{4,6},{6,4},{8,10},{10,8},{12,14},{14,12},{1,3},{3,1},... | collective-permute-start | bytes 319496 | tf_op jit(solution)/shard_map/ppermute | solution.py:35
  162.9 9.6 %collective-permute-done.17 = bf16[416,256]{1,0:T(8,128)(2,1)S(1)} collective-permute-done((bf16[416,256]{1,0:T(8,128)(2,1)S(1)}, bf16[416,256]{1,0:T(8,128)(2,1)S(1)}, u32[]{:S(2)}, u32[]{:S(2)}) %collective-permute-start.17) | collective-permute-done | bytes 213024 | tf_op jit(solution)/shard_map/ppermute | solution.py:35
  172.8 3.1 %multiply_convert_fusion.2 = bf16[2,2,2,256,256]{4,3,2,1,0:T(8,128)(2,1)} fusion(f32[2,2,2,256,256]{4,3,2,1,0:T(8,128)S(1)} %copy-done.4, f32[2,2,2,256,256]{4,3,2,1,0:T(8,128)S(1)} %fusion.5, bf16[2,2,2,256,256]{4,3,2,1,0:T(8,128)(2,1)S(1)} %broadcast_multiply_fusion.1, f32[2,2]{1,0:T(2,128)S(1)} %get-tuple-element.7, f32[2,2,256,256]{3,2,1,0:T(8,128)S(1)} %fusion.77, ...), kind=kOutput, calls=%fused_computation.23 | convolution fusion | flops 272105472 | bytes 8520704 | tf_op jit(solution)/shard_map/dot_general | solution.py:86
  175.9 5.7 %collective-permute-done.18 = bf16[832,256]{1,0:T(8,128)(2,1)S(1)} collective-permute-done((bf16[832,256]{1,0:T(8,128)(2,1)S(1)}, bf16[832,256]{1,0:T(8,128)(2,1)S(1)}, u32[]{:S(2)}, u32[]{:S(2)}) %collective-permute-start.18) | collective-permute-done | bytes 426016 | tf_op jit(solution)/shard_map/ppermute | solution.py:35
  181.9 2.2 %fusion.4 = bf16[2,2,2,256,256]{4,3,2,1,0:T(8,128)(2,1)} fusion(bf16[2,2,2,256,256]{4,3,2,1,0:T(8,128)(2,1)S(1)} %get-tuple-element.6, f32[2,2,2,256,256]{4,3,2,1,0:T(8,128)S(1)} %fusion.17, f32[2,2,2,256,256]{4,3,2,1,0:T(8,128)S(1)} %fusion.38, f32[2,2,2,256,256]{4,3,2,1,0:T(8,128)S(1)} %fusion.40, f32[2,2,2,256,256]{4,3,2,1,0:T(8,128)S(1)} %copy-done.5, ...), kind=kOutput, calls=%fused_computation.13 | convolution fusion | flops 275775488 | bytes 21104128 | tf_op jit(solution)/shard_map/dot_general | solution.py:79
  (111 shorter events, 47.7 us)
Async XLA Ops:
  0.6 123.7 %copy-start = (bf16[256,256]{1,0:T(8,128)(2,1)S(1)}, bf16[256,256]{1,0:T(8,128)(2,1)}, u32[]{:S(2)}) copy-start(bf16[256,256]{1,0:T(8,128)(2,1)} %param.11) | copy-start | bytes 393220
  1.4 6.9 %copy-start.15 = (bf16[2,2,2,256,256]{4,3,2,1,0:T(8,128)(2,1)S(1)}, bf16[2,2,2,256,256]{4,3,2,1,0:T(8,128)(2,1)}, u32[]{:S(2)}) copy-start(bf16[2,2,2,256,256]{4,3,2,1,0:T(8,128)(2,1)} %param.7) | copy-start | bytes 3145732
  3.9 16.9 %collective-permute-start = (bf16[2,2,1,256,256]{4,3,2,1,0:T(8,128)(2,1)}, bf16[2,2,1,256,256]{4,3,2,1,0:T(8,128)(2,1)}, u32[]{:S(2)}, u32[]{:S(2)}) collective-permute-start(bf16[2,2,1,256,256]{4,3,2,1,0:T(8,128)(2,1)} %get-tuple-element.11), channel_id=1, source_target_pairs={{0,1},{2,3},{4,5},{6,7},{8,9},{10,11},{12,13},{14,15},{16,17},{18,... | collective-permute-start | bytes 1572872 | tf_op jit(solution)/shard_map/ppermute | solution.py:62
  7.1 13.7 %collective-permute-start.1 = (bf16[2,2,1,256,256]{4,3,2,1,0:T(8,128)(2,1)}, bf16[2,2,1,256,256]{4,3,2,1,0:T(8,128)(2,1)}, u32[]{:S(2)}, u32[]{:S(2)}) collective-permute-start(bf16[2,2,1,256,256]{4,3,2,1,0:T(8,128)(2,1)} %get-tuple-element.12), channel_id=1, source_target_pairs={{1,0},{3,2},{5,4},{7,6},{9,8},{11,10},{13,12},{15,14},{17,16},{19,... | collective-permute-start | bytes 1572872 | tf_op jit(solution)/shard_map/ppermute | solution.py:62
  8.8 52.4 %copy-start.1 = (f32[2,2,256,256]{3,2,1,0:T(8,128)}, f32[2,2,256,256]{3,2,1,0:T(8,128)S(1)}, u32[]{:S(2)}) copy-start(f32[2,2,256,256]{3,2,1,0:T(8,128)S(1)} %get-tuple-element.5) | copy-start | bytes 3145732
  8.8 65.4 %collective-permute-start.6 = (bf16[2,2,2,256,256]{4,3,2,1,0:T(8,128)(2,1)S(1)}, bf16[2,2,2,256,256]{4,3,2,1,0:T(8,128)(2,1)}, u32[]{:S(2)}, u32[]{:S(2)}) collective-permute-start(bf16[2,2,2,256,256]{4,3,2,1,0:T(8,128)(2,1)S(1)} %get-tuple-element.6), channel_id=1, source_target_pairs={{2,0},{4,2},{6,4},{8,6},{10,8},{12,10},{14,12},{3,1},{5,3},{7,5},{... | collective-permute-start | bytes 3145736 | tf_op jit(solution)/shard_map/ppermute | solution.py:62
  10.9 37.8 %collective-permute-start.3 = (bf16[2,2,256,256]{3,2,1,0:T(8,128)(2,1)}, bf16[2,2,256,256]{3,2,1,0:T(8,128)(2,1)}, u32[]{:S(2)}, u32[]{:S(2)}) collective-permute-start(bf16[2,2,256,256]{3,2,1,0:T(8,128)(2,1)} %slice_bitcast_fusion), channel_id=1, source_target_pairs={{0,2},{1,3},{16,18},{17,19}} | collective-permute-start | bytes 1572872 | tf_op jit(solution)/shard_map/ppermute | solution.py:13
  17.5 43.7 %collective-permute-start.9 = (bf16[2,2,256,256]{3,2,1,0:T(8,128)(2,1)}, bf16[2,2,256,256]{3,2,1,0:T(8,128)(2,1)}, u32[]{:S(2)}, u32[]{:S(2)}) collective-permute-start(bf16[2,2,256,256]{3,2,1,0:T(8,128)(2,1)} %convert_element_type.107), channel_id=1, source_target_pairs={{8,0},{10,2},{12,4},{14,6},{9,1},{11,3},{13,5},{15,7},{24,16},{26,... | collective-permute-start | bytes 1572872 | tf_op jit(solution)/shard_map/ppermute | solution.py:27
  48.8 35.5 %collective-permute-start.4 = (bf16[2,2,256,256]{3,2,1,0:T(8,128)(2,1)S(1)}, bf16[2,2,256,256]{3,2,1,0:T(8,128)(2,1)S(1)}, u32[]{:S(2)}, u32[]{:S(2)}) collective-permute-start(bf16[2,2,256,256]{3,2,1,0:T(8,128)(2,1)S(1)} %broadcast_select_fusion), channel_id=1, source_target_pairs={{0,4},{2,6},{1,5},{3,7},{16,20},{18,22},{17,21},{19,23}} | collective-permute-start | bytes 1572872 | tf_op jit(solution)/shard_map/ppermute | solution.py:13
  62.3 35.1 %collective-permute-start.10 = (bf16[2,2,256,256]{3,2,1,0:T(8,128)(2,1)S(1)}, bf16[2,2,256,256]{3,2,1,0:T(8,128)(2,1)S(1)}, u32[]{:S(2)}, u32[]{:S(2)}) collective-permute-start(bf16[2,2,256,256]{3,2,1,0:T(8,128)(2,1)S(1)} %fusion.73), channel_id=1, source_target_pairs={{4,0},{6,2},{5,1},{7,3},{20,16},{22,18},{21,17},{23,19}} | collective-permute-start | bytes 1572872 | tf_op jit(solution)/shard_map/ppermute | solution.py:27
  68.9 90.9 %collective-permute-start.2 = (bf16[2,2,2,256,256]{4,3,2,1,0:T(8,128)(2,1)}, bf16[2,2,2,256,256]{4,3,2,1,0:T(8,128)(2,1)}, u32[]{:S(2)}, u32[]{:S(2)}) collective-permute-start(bf16[2,2,2,256,256]{4,3,2,1,0:T(8,128)(2,1)} %get-tuple-element.15), channel_id=1, source_target_pairs={{0,2},{2,4},{4,6},{6,8},{8,10},{10,12},{12,14},{1,3},{3,5},{5,7},{... | collective-permute-start | bytes 3145736 | tf_op jit(solution)/shard_map/ppermute | solution.py:62
  84.3 7.3 %copy-start.7 = (f32[1792,256]{1,0:T(8,128)}, f32[1792,256]{1,0:T(8,128)S(1)}, u32[]{:S(2)}) copy-start(f32[1792,256]{1,0:T(8,128)S(1)} %get-tuple-element.13) | copy-start | bytes 5505028
  84.4 23.7 %collective-permute-start.5 = (bf16[2,2,256,256]{3,2,1,0:T(8,128)(2,1)S(1)}, bf16[2,2,256,256]{3,2,1,0:T(8,128)(2,1)S(1)}, u32[]{:S(2)}, u32[]{:S(2)}) collective-permute-start(bf16[2,2,256,256]{3,2,1,0:T(8,128)(2,1)S(1)} %broadcast_select_fusion.1), channel_id=1, source_target_pairs={{0,8},{2,10},{4,12},{6,14},{1,9},{3,11},{5,13},{7,15},{16,24},{18,... | collective-permute-start | bytes 1572872 | tf_op jit(solution)/shard_map/ppermute | solution.py:13
  85.7 29.4 %collective-permute-start.8 = (bf16[2,2,1,256,256]{4,3,2,1,0:T(8,128)(2,1)}, bf16[2,2,1,256,256]{4,3,2,1,0:T(8,128)(2,1)}, u32[]{:S(2)}, u32[]{:S(2)}) collective-permute-start(bf16[2,2,1,256,256]{4,3,2,1,0:T(8,128)(2,1)} %get-tuple-element.9), channel_id=1, source_target_pairs={{1,0},{3,2},{5,4},{7,6},{9,8},{11,10},{13,12},{15,14},{17,16},{19,... | collective-permute-start | bytes 1572872 | tf_op jit(solution)/shard_map/ppermute | solution.py:62
  87.0 28.1 %collective-permute-start.7 = (bf16[2,2,1,256,256]{4,3,2,1,0:T(8,128)(2,1)}, bf16[2,2,1,256,256]{4,3,2,1,0:T(8,128)(2,1)}, u32[]{:S(2)}, u32[]{:S(2)}) collective-permute-start(bf16[2,2,1,256,256]{4,3,2,1,0:T(8,128)(2,1)} %get-tuple-element.10), channel_id=1, source_target_pairs={{0,1},{2,3},{4,5},{6,7},{8,9},{10,11},{12,13},{14,15},{16,17},{18,... | collective-permute-start | bytes 1572872 | tf_op jit(solution)/shard_map/ppermute | solution.py:62
  93.8 3.6 %copy-start.2 = (f32[2,2,256,256]{3,2,1,0:T(8,128)S(1)}, f32[2,2,256,256]{3,2,1,0:T(8,128)}, u32[]{:S(2)}) copy-start(f32[2,2,256,256]{3,2,1,0:T(8,128)} %copy-done.1) | copy-start | bytes 3145732
  97.4 6.1 %copy-start.11 = (bf16[2,2,256,256]{3,2,1,0:T(8,128)(2,1)}, bf16[2,2,256,256]{3,2,1,0:T(8,128)(2,1)S(1)}, u32[]{:S(2)}) copy-start(bf16[2,2,256,256]{3,2,1,0:T(8,128)(2,1)S(1)} %collective-permute-done.10) | copy-start | bytes 1572868
  99.7 24.6 %collective-permute-start.11 = (bf16[2,2,256,256]{3,2,1,0:T(8,128)(2,1)}, bf16[2,2,256,256]{3,2,1,0:T(8,128)(2,1)}, u32[]{:S(2)}, u32[]{:S(2)}) collective-permute-start(bf16[2,2,256,256]{3,2,1,0:T(8,128)(2,1)} %fusion.75), channel_id=1, source_target_pairs={{2,0},{3,1},{18,16},{19,17}} | collective-permute-start | bytes 1572872 | tf_op jit(solution)/shard_map/ppermute | solution.py:27
  115.0 4.1 %collective-permute-start.12 = (bf16[1664,256]{1,0:T(8,128)(2,1)S(1)}, bf16[1664,256]{1,0:T(8,128)(2,1)S(1)}, u32[]{:S(2)}, u32[]{:S(2)}) collective-permute-start(bf16[1664,256]{1,0:T(8,128)(2,1)S(1)} %select_convert_fusion), channel_id=1, source_target_pairs={{0,1},{1,0},{2,3},{3,2},{4,5},{5,4},{6,7},{7,6},{8,9},{9,8},{10,11... | collective-permute-start | bytes 2555912 | tf_op jit(solution)/shard_map/ppermute | solution.py:35
  120.9 3.4 %copy-start.3 = (f32[2,2,256,256]{3,2,1,0:T(8,128)S(1)}, f32[2,2,256,256]{3,2,1,0:T(8,128)}, u32[]{:S(2)}) copy-start(f32[2,2,256,256]{3,2,1,0:T(8,128)} %copy-done.1) | copy-start | bytes 3145732
  120.9 3.4 %copy-start.12 = (bf16[2,2,256,256]{3,2,1,0:T(8,128)(2,1)S(1)}, bf16[2,2,256,256]{3,2,1,0:T(8,128)(2,1)}, u32[]{:S(2)}) copy-start(bf16[2,2,256,256]{3,2,1,0:T(8,128)(2,1)} %copy-done.11) | copy-start | bytes 1572868
  121.0 13.1 %collective-permute-start.13 = (bf16[832,256]{1,0:T(8,128)(2,1)S(1)}, bf16[832,256]{1,0:T(8,128)(2,1)S(1)}, u32[]{:S(2)}, u32[]{:S(2)}) collective-permute-start(bf16[832,256]{1,0:T(8,128)(2,1)S(1)} %select_convert_fusion.1), channel_id=1, source_target_pairs={{0,4},{2,6},{4,0},{6,2},{8,12},{10,14},{12,8},{14,10},{1,5},{3,7},... | collective-permute-start | bytes 1277960 | tf_op jit(solution)/shard_map/ppermute | solution.py:35
  134.3 13.2 %collective-permute-start.14 = (bf16[416,256]{1,0:T(8,128)(2,1)S(1)}, bf16[416,256]{1,0:T(8,128)(2,1)S(1)}, u32[]{:S(2)}, u32[]{:S(2)}) collective-permute-start(bf16[416,256]{1,0:T(8,128)(2,1)S(1)} %select_convert_fusion.2), channel_id=1, source_target_pairs={{0,8},{2,10},{4,12},{6,14},{8,0},{10,2},{12,4},{14,6},{1,9},{3,11}... | collective-permute-start | bytes 638984 | tf_op jit(solution)/shard_map/ppermute | solution.py:35
  147.6 12.1 %copy-start.14 = (bf16[3,256,256]{2,1,0:T(8,128)(2,1)S(1)}, bf16[3,256,256]{2,1,0:T(8,128)(2,1)}, u32[]{:S(2)}) copy-start(bf16[3,256,256]{2,1,0:T(8,128)(2,1)} %param.10) | copy-start | bytes 1179652
  147.6 10.0 %collective-permute-start.15 = (bf16[208,256]{1,0:T(8,128)(2,1)S(1)}, bf16[208,256]{1,0:T(8,128)(2,1)S(1)}, u32[]{:S(2)}, u32[]{:S(2)}) collective-permute-start(bf16[208,256]{1,0:T(8,128)(2,1)S(1)} %select_convert_fusion.3), channel_id=1, source_target_pairs={{0,2},{2,0},{4,6},{6,4},{8,10},{10,8},{12,14},{14,12},{1,3},{3,1},... | collective-permute-start | bytes 319496 | tf_op jit(solution)/shard_map/ppermute | solution.py:35
  157.7 4.9 %copy-start.6 = (bf16[2,2,256,256]{3,2,1,0:T(8,128)(2,1)S(1)}, bf16[2,2,256,256]{3,2,1,0:T(8,128)(2,1)}, u32[]{:S(2)}) copy-start(bf16[2,2,256,256]{3,2,1,0:T(8,128)(2,1)} %broadcast_select_fusion.2) | copy-start | bytes 1572868
  157.7 4.8 %collective-permute-start.16 = (bf16[208,256]{1,0:T(8,128)(2,1)S(1)}, bf16[208,256]{1,0:T(8,128)(2,1)S(1)}, u32[]{:S(2)}, u32[]{:S(2)}) collective-permute-start(bf16[208,256]{1,0:T(8,128)(2,1)S(1)} %add_convert_fusion), channel_id=1, source_target_pairs={{0,2},{2,0},{4,6},{6,4},{8,10},{10,8},{12,14},{14,12},{1,3},{3,1},... | collective-permute-start | bytes 319496 | tf_op jit(solution)/shard_map/ppermute | solution.py:35
  161.4 11.4 %copy-start.4 = (f32[2,2,2,256,256]{4,3,2,1,0:T(8,128)S(1)}, f32[2,2,2,256,256]{4,3,2,1,0:T(8,128)}, u32[]{:S(2)}) copy-start(f32[2,2,2,256,256]{4,3,2,1,0:T(8,128)} %fusion.112) | copy-start | bytes 6291460
  162.5 10.0 %collective-permute-start.17 = (bf16[416,256]{1,0:T(8,128)(2,1)S(1)}, bf16[416,256]{1,0:T(8,128)(2,1)S(1)}, u32[]{:S(2)}, u32[]{:S(2)}) collective-permute-start(bf16[416,256]{1,0:T(8,128)(2,1)S(1)} %maximum_select_fusion.3), channel_id=1, source_target_pairs={{0,8},{2,10},{4,12},{6,14},{8,0},{10,2},{12,4},{14,6},{1,9},{3,11}... | collective-permute-start | bytes 638984 | tf_op jit(solution)/shard_map/ppermute | solution.py:35
  172.7 8.9 %collective-permute-start.18 = (bf16[832,256]{1,0:T(8,128)(2,1)S(1)}, bf16[832,256]{1,0:T(8,128)(2,1)S(1)}, u32[]{:S(2)}, u32[]{:S(2)}) collective-permute-start(bf16[832,256]{1,0:T(8,128)(2,1)S(1)} %maximum_select_fusion.2), channel_id=1, source_target_pairs={{0,4},{2,6},{4,0},{6,2},{8,12},{10,14},{12,8},{14,10},{1,5},{3,7},... | collective-permute-start | bytes 1277960 | tf_op jit(solution)/shard_map/ppermute | solution.py:35
  172.8 9.2 %copy-start.5 = (f32[2,2,2,256,256]{4,3,2,1,0:T(8,128)S(1)}, f32[2,2,2,256,256]{4,3,2,1,0:T(8,128)}, u32[]{:S(2)}) copy-start(f32[2,2,2,256,256]{4,3,2,1,0:T(8,128)} %fusion.91) | copy-start | bytes 6291460
  181.8 2.4 %collective-permute-start.19 = (bf16[1664,256]{1,0:T(8,128)(2,1)S(1)}, bf16[1664,256]{1,0:T(8,128)(2,1)S(1)}, u32[]{:S(2)}, u32[]{:S(2)}) collective-permute-start(bf16[1664,256]{1,0:T(8,128)(2,1)S(1)} %maximum_select_fusion.1), channel_id=1, source_target_pairs={{0,1},{1,0},{2,3},{3,2},{4,5},{5,4},{6,7},{7,6},{8,9},{9,8},{10,11... | collective-permute-start | bytes 2555912 | tf_op jit(solution)/shard_map/ppermute | solution.py:35
  (4 other events, 8.1 us)

commit v2 on v0

v2 whole, which is shorter than its diff:
```python
import functools

import jax
import jax.numpy as jnp
from jax import lax
from jax.experimental import pallas as pl
from jax.experimental.pallas import tpu as pltpu
from jax.sharding import PartitionSpec as P

MESH = pl.DeviceIdType.MESH
BF = jnp.bfloat16
F32 = jnp.float32


def nn(left, right):
    return jnp.dot(left, right, preferred_element_type=F32)


def nt(left, right):
    return lax.dot_general(left, right, (((1,), (1,)), ((), ())), preferred_element_type=F32)


def bits_of(count):
    far = []
    bit = 2
    while bit < count:
        far.append(bit)
        bit *= 2
    return far + ([1] if count > 1 else [])


def kernel(n, dims, scale, *refs):
    clips, frames, rows, cols, chans, sizes = dims
    (lat, cotan, mask, sw, tw, cw, out, glat, gsp, gtm, gcd,
     xm, xh, x3, xt, pre, actp, at, cotp, dm, dh, fst, ft, csum, cs, cr, cb,
     acc, tmr, xs, xr, ms, zs, zr, res,
     halo_sem, cot_sem, act_sem, first_sem, sum_sem, tm_sem, x_sem, z_send, z_recv,
     g_send, g_recv, xg_sem, tg_sem) = refs
    d3 = x3
    group = lax.axis_index("groups")
    s = lax.axis_index("space")
    c = lax.axis_index("tm")
    half = n // 2
    xb = lax.rem(s, 2)
    q = lax.div(s, 2)
    pos = rows * cols
    order = bits_of(n)
    levels = len(order)

    def at_dev(space, core):
        return (group, space, core)

    def copy(src, dst, sems, dev):
        return pltpu.make_async_remote_copy(
            src_ref=src, dst_ref=dst, send_sem=sems[0], recv_sem=sems[1],
            device_id=dev, device_id_type=MESH)

    def pair(sem, *index):
        return sem.at[(0,) + index], sem.at[(1,) + index]

    partner = at_dev(s, 1 - c)
    side = at_dev(s + 1 - 2 * xb, c)

    barrier = pltpu.get_barrier_semaphore()
    pl.semaphore_signal(barrier, inc=1, device_id=partner, device_id_type=MESH)
    for d in range(1, n):
        pl.semaphore_signal(
            barrier, inc=1, device_id=at_dev(lax.rem(s + d, n), c), device_id_type=MESH)
    pl.semaphore_wait(barrier, n)

    def mask_of(b, t):
        return mask[b * frames + t]

    for b in range(clips):
        for t in range(frames):
            cotp[b, t] = (cotan[b, t].astype(F32) * mask_of(b, t)).astype(BF)

    def cot_copy(b):
        return copy(cotp.at[b, pl.ds(0, frames)], cotp.at[b, pl.ds(frames, frames)],
                    pair(cot_sem, b), at_dev(jnp.maximum(s - 1, 0), c))

    def act_copy(b):
        return copy(actp.at[b, pl.ds(frames, frames)], actp.at[b, pl.ds(0, frames)],
                    pair(act_sem, b), at_dev(jnp.minimum(s + 1, n - 1), c))

    @pl.when(s > 0)
    def _():
        for b in range(clips):
            cot_copy(b).start()

    for b in range(clips):
        for t in range(frames):
            xm[b * frames + t] = (lat[b, t].astype(F32) * mask_of(b, t)).astype(BF)

    edge = pl.ds(pl.multiple_of((1 - c) * (rows - 1) * cols, cols), cols)
    x_halo = copy(xm.at[:, edge], xh, pair(halo_sem, 0), partner)
    x_halo.start()
    d_halo = copy(dm.at[:, edge], dh, pair(halo_sem, 1), partner)

    def clear(upto):
        held = jnp.bool_(True)
        for bit in upto:
            held = held & (lax.rem(lax.div(s, bit), 2) == 0)
        return held

    def has(bit):
        return lax.rem(lax.div(s, bit), 2) == 1

    out_order = order[::-1]

    def first_copy(level):
        bit = out_order[level]
        return copy(fst, fst, pair(first_sem, level), at_dev(jnp.minimum(s + bit, n - 1), c))

    def first_send(level):
        @pl.when(clear(out_order[level:]))
        def _():
            first_copy(level).start()

    def first_recv(level):
        @pl.when(has(out_order[level]) & clear(out_order[level + 1:]))
        def _():
            first_copy(level).wait_recv()

    def first_done(level):
        @pl.when(clear(out_order[level:]))
        def _():
            first_copy(level).wait_send()

    def sum_copy(level):
        return copy(cs, cr.at[level], pair(sum_sem, level),
                    at_dev(jnp.maximum(s - order[level], 0), c))

    def sum_send(level):
        @pl.when(has(order[level]) & clear(order[:level]))
        def _():
            cs[...] = csum[...].astype(BF)
            sum_copy(level).start()

    def sum_recv(level):
        @pl.when(clear(order[:level + 1]))
        def _():
            sum_copy(level).wait_recv()
            csum[...] += cr[level].astype(F32)

    def sum_done(level):
        @pl.when(has(order[level]) & clear(order[:level]))
        def _():
            sum_copy(level).wait_send()

    @pl.when(s == 0)
    def _():
        for b in range(clips):
            fst[b] = xm[b * frames]

    first_send(0)
    for b in range(clips):
        total = cotp[b, 0].astype(F32)
        for t in range(1, frames):
            total += cotp[b, t].astype(F32)
        csum[b] = total
    sum_send(0)

    @pl.when(s == n - 1)
    def _():
        cotp[:, frames:] = jnp.zeros((clips, frames, pos, chans), BF)

    @pl.when(s == 0)
    def _():
        actp[:, :frames] = jnp.zeros((clips, frames, pos, chans), BF)

    ids = lax.broadcasted_iota(jnp.int32, (cols, chans), 0)

    def spread(dst, bt, block, value, flip):
        wide = value.astype(F32)
        prev = jnp.where(ids == 0, 0.0, pltpu.roll(wide, 1, 0)).astype(BF)
        nxt = jnp.where(ids == cols - 1, 0.0, pltpu.roll(wide, cols - 1, 0)).astype(BF)
        span = pl.ds(pl.multiple_of(block * cols, cols), cols)
        lo, hi = (nxt, prev) if flip else (prev, nxt)
        dst[bt, span, 0:chans] = lo
        dst[bt, span, chans:2 * chans] = value
        dst[bt, span, 2 * chans:3 * chans] = hi

    def spread_own(dst, src, flip):
        @pl.loop(0, clips * frames)
        def _(bt):
            for r in range(rows):
                spread(dst, bt, r + 1, src[bt, r * cols:(r + 1) * cols], flip)

    def spread_halo(dst, src, flip):
        @pl.loop(0, clips * frames)
        def _(bt):
            got = src[bt].astype(F32)
            spread(dst, bt, 0, (got * c.astype(F32)).astype(BF), flip)
            spread(dst, bt, rows + 1, (got * (1 - c).astype(F32)).astype(BF), flip)

    spread_own(x3, xm, False)

    @pl.loop(0, clips * frames)
    def _(bt):
        xt[bt] = xm[bt].T

    x_halo.wait()
    spread_halo(x3, xh, False)

    for b in range(clips):
        @pl.loop(0, frames)
        def _(t):
            bt = b * frames + t
            total = nn(x3[bt, 0:pos], sw[0])
            for i in range(1, 3):
                total += nn(x3[bt, i * cols:i * cols + pos], sw[i])
            pre[bt] = total
            act = (total * jax.nn.sigmoid(total)).astype(BF)
            actp[b, frames + t] = act
            at[bt] = act.T

    first_recv(0)
    if levels > 1:
        first_send(1)
    sum_recv(0)
    if levels > 1:
        sum_send(1)

    for b in range(clips):
        @pl.when(s < n - 1)
        def _():
            cot_copy(b).wait_recv()

        @pl.when(s < n - 1)
        def _():
            act_copy(b).start()

        @pl.loop(0, frames)
        def _(t):
            bt = b * frames + t
            dact = nt(cotp[b, t], tw[0])
            for k in range(1, 3):
                dact += nt(cotp[b, t + k], tw[k])
            value = pre[bt]
            sig = jax.nn.sigmoid(value)
            dm[bt] = (dact * sig * (1.0 + value * (1.0 - sig))).astype(BF)

    d_halo.start()
    for level in range(1, levels):
        first_recv(level)
        if level + 1 < levels:
            first_send(level + 1)

    base = [sum(sizes[:k]) for k in range(len(sizes))]

    def part(k, div, index, count):
        size = sizes[k] // div
        return pl.ds(pl.multiple_of(index * size, 16), size * count)

    def shift(k, div, offset):
        size = sizes[k] // div
        return pl.ds(pl.multiple_of(base[k] // div + offset, 16), size)

    def tm_copy(k):
        size = sizes[k] // 2
        src = acc.at[pl.ds(pl.multiple_of(base[k] + (1 - c) * size, 16), size)]
        return copy(src, tmr.at[pl.ds(base[k] // 2, size)], pair(tm_sem, k), partner)

    def x_copy(k):
        span = pl.ds(base[k] // 4, sizes[k] // 4)
        return copy(xs.at[span], xr.at[span], pair(x_sem, k), side)

    def z_peer(d):
        other = lax.rem(q + d, half)
        return other, at_dev(2 * other + xb, c)

    def z_copy(k, d):
        size = sizes[k] // (2 * n)
        other, dev = z_peer(d)
        src = zs.at[pl.ds(pl.multiple_of(base[k] // 4 + other * size, 16), size)]
        dst = zr.at[d - 1, pl.ds(base[k] // (2 * n), size)]
        return copy(src, dst, (z_send.at[k, d - 1], z_recv.at[k, d - 1]), dev)

    def quarter(k):
        return base[k] + c * (sizes[k] // 2) + xb * (sizes[k] // 4)

    def g_copy(k, d, place):
        size = sizes[k] // (2 * n)
        own = res.at[pl.ds(pl.multiple_of(quarter(k) + place * size, 16), size)]
        return copy(own, own, (g_send.at[k, d - 1], g_recv.at[k, d - 1]), z_peer(d)[1])

    def xg_copy(k, bit):
        size = sizes[k] // 4
        start = base[k] + c * (sizes[k] // 2) + bit * size
        own = res.at[pl.ds(pl.multiple_of(start, 16), size)]
        return copy(own, own, pair(xg_sem, k), side)

    def tg_copy(k, bit):
        size = sizes[k] // 2
        own = res.at[pl.ds(pl.multiple_of(base[k] + bit * size, 16), size)]
        return copy(own, own, pair(tg_sem, k), partner)

    def stage_x(k):
        tm_copy(k).wait_recv()
        size = sizes[k] // 4
        away = (1 - xb) * size
        xs[pl.ds(base[k] // 4, size)] = (
            acc[pl.ds(pl.multiple_of(base[k] + c * 2 * size + away, 16), size)]
            + tmr[pl.ds(pl.multiple_of(base[k] // 2 + away, 16), size)]).astype(BF)
        x_copy(k).start()

    def stage_z(k):
        x_copy(k).wait_recv()
        size = sizes[k] // 4
        span = pl.ds(base[k] // 4, size)
        total = (acc[pl.ds(pl.multiple_of(quarter(k), 16), size)]
                 + tmr[pl.ds(pl.multiple_of(base[k] // 2 + xb * size, 16), size)]
                 + xr[span].astype(F32))
        ms[span] = total
        zs[span] = total.astype(BF)
        for d in range(1, half):
            z_copy(k, d).start()

    def stage_g(k):
        size = sizes[k] // (2 * n)
        total = ms[pl.ds(pl.multiple_of(base[k] // 4 + q * size, 16), size)]
        for d in range(1, half):
            z_copy(k, d).wait_recv()
            total += zr[d - 1, pl.ds(base[k] // (2 * n), size)].astype(F32)
        res[pl.ds(pl.multiple_of(quarter(k) + q * size, 16), size)] = (total * scale).astype(BF)
        for d in range(1, half):
            g_copy(k, d, q).start()

    def stage_xg(k):
        for d in range(1, half):
            g_copy(k, d, lax.rem(q + half - d, half)).wait_recv()
        xg_copy(k, xb).start()

    def stage_tg(k):
        xg_copy(k, 1 - xb).wait_recv()
        tg_copy(k, c).start()

    def stage_end(k):
        tg_copy(k, 1 - c).wait_recv()

    def write_tap(k, tap, value):
        acc[base[k] + tap * chans:base[k] + (tap + 1) * chans] = value

    for b in range(clips):
        ft[b] = fst[b].T
    for k in range(3):
        total = jnp.zeros((chans, chans), F32)
        for b in range(clips):
            for t in range(frames):
                total += nn(at[b * frames + t], cotp[b, t + k])
        write_tap(0, k, total)
    total = jnp.zeros((chans, chans), F32)
    for b in range(clips):
        for t in range(frames):
            total += nn(ft[b], cotp[b, t])
    write_tap(0, 3, total)
    for k in range(4):
        used = (4 if k == 0 else 3) * chans
        if sizes[k] > used:
            acc[base[k] + used:base[k] + sizes[k]] = jnp.zeros((sizes[k] - used, chans), F32)
    tm_copy(0).start()

    spread_own(d3, dm, True)
    d_halo.wait()
    spread_halo(d3, dh, True)
    stage_x(0)

    def spatial_grad(i):
        for j in range(3):
            total = jnp.zeros((chans, chans), F32)
            for bt in range(clips * frames):
                piece = d3[bt, (2 - i) * cols:(2 - i) * cols + pos, j * chans:(j + 1) * chans]
                total += nn(xt[bt], piece)
            write_tap(1 + i, j, total)
        tm_copy(1 + i).start()

    spatial_grad(0)
    stage_z(0)
    spatial_grad(1)
    stage_x(1)
    spatial_grad(2)
    stage_x(2)
    stage_z(1)
    stage_x(3)
    stage_g(0)
    stage_z(2)

    for level in range(1, levels):
        sum_recv(level)
        if level + 1 < levels:
            sum_send(level + 1)

    @pl.when(s == 0)
    def _():
        for b in range(clips):
            high = csum[b].astype(BF)
            low = (csum[b] - high.astype(F32)).astype(BF)
            cb[b] = nt(high, cw[...]) + nt(low, cw[...])

    @pl.when(s > 0)
    def _():
        cb[...] = jnp.zeros((clips, pos, chans), F32)

    def back(b, t):
        bt = b * frames + t
        total = cotp[b, t].astype(F32)
        for i in range(3):
            for j in range(3):
                piece = d3[bt, (2 - i) * cols:(2 - i) * cols + pos, j * chans:(j + 1) * chans]
                total += nt(piece, sw[i, j * chans:(j + 1) * chans])
        if t == 0:
            total += cb[b]
        glat[b, t] = (total * mask_of(b, t)).astype(BF)

    stage_z(3)
    stage_g(1)
    for b in range(clips):
        for t in range(frames):
            back(b, t)
    stage_xg(0)
    stage_g(2)
    stage_g(3)
    stage_xg(1)
    stage_tg(0)

    for b in range(clips):
        @pl.when(s > 0)
        def _():
            act_copy(b).wait_recv()
        cond = nn(fst[b], cw[...])
        for t in range(frames):
            total = xm[b * frames + t].astype(F32) + cond
            for k in range(3):
                total += nn(actp[b, frames + t - k], tw[k])
            out[b, t] = (total * mask_of(b, t)).astype(BF)

    stage_xg(2)
    stage_tg(1)
    stage_xg(3)
    stage_tg(2)
    stage_tg(3)
    for k in range(4):
        stage_end(k)
    gtm[...] = res[0:3 * chans]
    gcd[...] = res[3 * chans:4 * chans]
    for i in range(3):
        gsp[i * 3 * chans:(i + 1) * 3 * chans] = res[base[1 + i]:base[1 + i] + 3 * chans]

    for level in range(levels):
        first_done(level)
        sum_done(level)

    @pl.when(s > 0)
    def _():
        for b in range(clips):
            cot_copy(b).wait_send()

    @pl.when(s < n - 1)
    def _():
        for b in range(clips):
            act_copy(b).wait_send()

    for k in range(4):
        tm_copy(k).wait_send()
        x_copy(k).wait_send()
        for d in range(1, half):
            z_copy(k, d).wait_send()
            g_copy(k, d, q).wait_send()
        xg_copy(k, xb).wait_send()
        tg_copy(k, c).wait_send()


def on_device(latents, cotangent, valid_frames, spatial_weight, temporal_weight, cond_weight):
    clips, frames, rows, cols, chans = latents.shape
    n = lax.axis_size("space")
    slab = lax.axis_index("space")
    frame_ids = slab * frames + jnp.arange(frames, dtype=jnp.int32)
    mask = (frame_ids[None, :] < valid_frames[:, None]).astype(F32).reshape(clips * frames)
    scale = (clips * frames * rows * cols * n * lax.axis_size("tm")) ** (-0.5)
    pos = rows * cols
    unit = 32 * n
    sizes = [-(-taps * chans // unit) * unit for taps in (4, 3, 3, 3)]
    total = sum(sizes)
    bt = clips * frames
    levels = len(bits_of(n))
    half = n // 2
    dma = pltpu.SemaphoreType.DMA
    big = (clips, frames, pos, chans)
    scratch = [
        pltpu.VMEM((bt, pos, chans), BF),
        pltpu.VMEM((bt, cols, chans), BF),
        pltpu.VMEM((bt, pos + 2 * cols, 3 * chans), BF),
        pltpu.VMEM((bt, chans, pos), BF),
        pltpu.VMEM((bt, pos, chans), F32),
        pltpu.VMEM((clips, 2 * frames, pos, chans), BF),
        pltpu.VMEM((bt, chans, pos), BF),
        pltpu.VMEM((clips, 2 * frames, pos, chans), BF),
        pltpu.VMEM((bt, pos, chans), BF),
        pltpu.VMEM((bt, cols, chans), BF),
        pltpu.VMEM((clips, pos, chans), BF),
        pltpu.VMEM((clips, chans, pos), BF),
        pltpu.VMEM((clips, pos, chans), F32),
        pltpu.VMEM((clips, pos, chans), BF),
        pltpu.VMEM((levels, clips, pos, chans), BF),
        pltpu.VMEM((clips, pos, chans), F32),
        pltpu.VMEM((total, chans), F32),
        pltpu.VMEM((total // 2, chans), F32),
        pltpu.VMEM((total // 4, chans), BF),
        pltpu.VMEM((total // 4, chans), BF),
        pltpu.VMEM((total // 4, chans), F32),
        pltpu.VMEM((total // 4, chans), BF),
        pltpu.VMEM((half - 1, total // (2 * n), chans), BF),
        pltpu.VMEM((total, chans), BF),
        dma((2, 2)), dma((2, clips)), dma((2, clips)), dma((2, levels)), dma((2, levels)),
        dma((2, 4)), dma((2, 4)), dma((4, half - 1)), dma((4, half - 1)),
        dma((4, half - 1)), dma((4, half - 1)), dma((2, 4)), dma((2, 4)),
    ]
    vmem = pl.BlockSpec(memory_space=pltpu.VMEM)
    smem = pl.BlockSpec(memory_space=pltpu.SMEM)
    shape = jax.ShapeDtypeStruct
    outs = pl.pallas_call(
        functools.partial(kernel, n, (clips, frames, rows, cols, chans, sizes), scale),
        out_shape=[
            shape(big, BF), shape(big, BF), shape((9 * chans, chans), BF),
            shape((3 * chans, chans), BF), shape((chans, chans), BF)],
        in_specs=[vmem, vmem, smem, vmem, vmem, vmem],
        out_specs=[vmem] * 5,
        scratch_shapes=scratch,
        compiler_params=pltpu.CompilerParams(
            collective_id=0, has_side_effects=True, vmem_limit_bytes=58 * 2**20),
    )(
        latents.reshape(big), cotangent.reshape(big), mask,
        spatial_weight.reshape(3, 3 * chans, chans), temporal_weight, cond_weight)
    output, grad_latents, grad_spatial, grad_temporal, grad_cond = outs
    return (
        output.reshape(latents.shape), grad_latents.reshape(latents.shape),
        grad_spatial.reshape(9, chans, chans), grad_temporal.reshape(3, chans, chans), grad_cond)


def solution(mesh):
    return jax.shard_map(
        on_device,
        mesh=mesh,
        in_specs=(
            P("groups", "space", "tm", None, None),
            P("groups", "space", "tm", None, None),
            P("groups"),
            P(),
            P(),
            P(),
        ),
        out_specs=(
            P("groups", "space", "tm", None, None),
            P("groups", "space", "tm", None, None),
            P("groups", None, None),
            P("groups", None, None),
            P("groups", None),
        ),
        check_vma=False,
    )
```

time: 339 us -> 139 us (0.41)
  waiting for transfers between devices: 255 us -> 0 us
  Pallas kernels: 0 us -> 130 us
  matrix products: 42.3 us -> 0 us
  between operations: 15.5 us -> 0.67 us
  other arithmetic: 11.2 us -> 0.73 us
  starting transfers between devices: 5.03 us -> 0 us
    psum x3 -> x0, waiting for transfers between devices: 247 us -> none  [the longest x1 91.7 us: on_device(): lax.psum((spatial_terms, temporal_terms, cond_terms), ('space', 'tm'))]
    pallas_call x0 -> x1, Pallas kernels: none -> 130 us  [on_device(): pl.pallas_call(functools.partial(kernel, n, (clips, frames, rows, cols, c...]
    dot_general x39 -> x0, matrix products: 42.3 us -> none  [the longest x9 11.9 us: on_device(): lax.dot_general(piece, dpre, dims, preferred_element_type=jnp.float32)]
    ppermute x2 -> x0, waiting for transfers between devices: 7.84 us -> none  [shifted(): return lax.ppermute(value, axis, pairs)]
    ppermute x2 -> x0, starting transfers between devices: 4.83 us -> none  [shifted(): return lax.ppermute(value, axis, pairs)]
    convert_element_type x5 -> x1, other arithmetic: 5.27 us -> 0.73 us  [on_device(): (frame_ids[None, :] < valid_frames[:, None]).astype(F32)]
    dynamic_slice x2 -> x0, local copies, waits for them, and re-layouts: 3.6 us -> none  [own_window(): return lax.dynamic_slice_in_dim(padded_rows, start, rows + 2, 2)]
  transfers between devices with their start and end apart: 7 -> 0, of which waited for: 4 -> 0; matrix products, arithmetic and copies ran while one was open for 12% -> 0% of each run, Pallas kernels for 0% -> 0%
where the time goes in v2:
time: 139 us
  Pallas kernels  130 us (94%)
  local copies, waits for them, and re-layouts  7.23 us (5%)
    pallas_call x1, Pallas kernels, on_device(): pl.pallas_call(functools.partial(kernel, n, (clips, frames, rows, cols, c...  130 us
    unnamed x13, local copies, waits for them, and re-layouts  6.64 us

profile of v2, /device:TPU:0, one launch (start us, length us, event | category | flops | bytes accessed | tf_op | source)
XLA Modules:
  0.0 138.9 jit_solution(7166227365971361017)
XLA Ops:
  0.6 0.7 compare_convert_fusion
  1.4 0.6 reshape.49.refs_2_
  2.0 130.3 %shard_map.101 = (bf16[2,2,512,256]{3,2,1,0:T(8,128)(2,1)}, bf16[2,2,512,256]{3,2,1,0:T(8,128)(2,1)}, bf16[2304,256]{1,0:T(8,128)(2,1)}, bf16[768,256]{1,0:T(8,128)(2,1)}, bf16[256,256]{1,0:T(8,128)(2,1)}) custom-call(bf16[2,2,512,256]{3,2,1,0:T(8,128)(2,1)} %bitcast.11, bf16[2,2,512,256]{3,2,1,0:T(8,128)(2,1)} %bitcast.12, f32[4]{0:T(128)} %reshape.49.refs_2_, ...), custom_call_target="tpu_custom_call" | custom-call | tf_op jit(solution)/shard_map/pallas_call | solution.py:522
  132.3 0.0 copy-start.1
  132.3 2.4 %copy.16 = bf16[2,2,2,256,256]{4,3,2,1,0:T(8,128)(2,1)} copy(bf16[2,2,2,256,256]{4,3,2,1,0:T(8,128)(2,1)} %bitcast.10) | data formatting | bytes 2097152
  134.6 0.0 copy-done.1
  134.6 0.0 copy-start
  134.6 1.0 copy.17
  135.6 0.7 copy-done
  136.3 0.0 copy-start.2
  136.3 0.0 copy-start.3
  136.3 1.0 copy.18
  137.3 0.2 copy-done.2
  137.5 0.7 copy.19
  138.3 0.0 copy-done.3
  138.3 0.7 copy.20
  (1 shorter events, 0.0 us)
Async XLA Ops:
  132.3 2.4 %copy-start.1 = (bf16[2,2,512,256]{3,2,1,0:T(8,128)(2,1)S(1)}, bf16[2,2,512,256]{3,2,1,0:T(8,128)(2,1)}, u32[]{:S(2)}) copy-start(bf16[2,2,512,256]{3,2,1,0:T(8,128)(2,1)} %get-tuple-element.11) | copy-start | bytes 3145732
  134.6 1.6 %copy-start = (bf16[2304,256]{1,0:T(8,128)(2,1)S(1)}, bf16[2304,256]{1,0:T(8,128)(2,1)}, u32[]{:S(2)}) copy-start(bf16[2304,256]{1,0:T(8,128)(2,1)} %get-tuple-element.12) | copy-start | bytes 3538948
  136.3 1.2 copy-start.2
  136.3 2.0 %copy-start.3 = (bf16[256,256]{1,0:T(8,128)(2,1)S(1)}, bf16[256,256]{1,0:T(8,128)(2,1)}, u32[]{:S(2)}) copy-start(bf16[256,256]{1,0:T(8,128)(2,1)} %get-tuple-element.24) | copy-start | bytes 393220

commit v3 on v2

--- a/solution.py
+++ b/solution.py
@@ -95,7 +95,10 @@
     edge = pl.ds(pl.multiple_of((1 - c) * (rows - 1) * cols, cols), cols)
     x_halo = copy(xm.at[:, edge], xh, pair(halo_sem, 0), partner)
     x_halo.start()
-    d_halo = copy(dm.at[:, edge], dh, pair(halo_sem, 1), partner)
+
+    def d_halo(b):
+        span = pl.ds(b * frames, frames)
+        return copy(dm.at[span, edge], dh.at[span], pair(halo_sem, 1 + b), partner)
 
     def clear(upto):
         held = jnp.bool_(True)
@@ -108,58 +111,70 @@
 
     out_order = order[::-1]
 
-    def first_copy(level):
-        bit = out_order[level]
-        return copy(fst, fst, pair(first_sem, level), at_dev(jnp.minimum(s + bit, n - 1), c))
-
-    def first_send(level):
+    def first_copy(level, b):
+        return copy(fst.at[b], fst.at[b], pair(first_sem, level, b),
+                    at_dev(jnp.minimum(s + out_order[level], n - 1), c))
+
+    def first_send(level, b):
         @pl.when(clear(out_order[level:]))
         def _():
-            first_copy(level).start()
-
-    def first_recv(level):
+            first_copy(level, b).start()
+
+    def first_recv(level, b):
         @pl.when(has(out_order[level]) & clear(out_order[level + 1:]))
         def _():
-            first_copy(level).wait_recv()
-
-    def first_done(level):
+            first_copy(level, b).wait_recv()
+
+    def first_done(level, b):
         @pl.when(clear(out_order[level:]))
         def _():
-            first_copy(level).wait_send()
-
-    def sum_copy(level):
-        return copy(cs, cr.at[level], pair(sum_sem, level),
+            first_copy(level, b).wait_send()
+
+    def sum_copy(level, b):
+        return copy(cs.at[b], cr.at[level, b], pair(sum_sem, level, b),
                     at_dev(jnp.maximum(s - order[level], 0), c))
 
-    def sum_send(level):
+    def sum_send(level, b):
         @pl.when(has(order[level]) & clear(order[:level]))
         def _():
-            cs[...] = csum[...].astype(BF)
-            sum_copy(level).start()
-
-    def sum_recv(level):
+            cs[b] = csum[b].astype(BF)
+            sum_copy(level, b).start()
+
+    def sum_recv(level, b):
         @pl.when(clear(order[:level + 1]))
         def _():
-            sum_copy(level).wait_recv()
-            csum[...] += cr[level].astype(F32)
-
-    def sum_done(level):
+            sum_copy(level, b).wait_recv()
+            csum[b] += cr[level, b].astype(F32)
+
+    def sum_done(level, b):
         @pl.when(has(order[level]) & clear(order[:level]))
         def _():
-            sum_copy(level).wait_send()
+            sum_copy(level, b).wait_send()
+
+    hops = sorted(((level, b) for level in range(levels) for b in range(clips)),
+                  key=lambda hop: (hop[0] + hop[1], hop[0]))
+
+    def serve(count):
+        for _ in range(min(count, len(hops))):
+            level, b = hops.pop(0)
+            first_recv(level, b)
+            sum_recv(level, b)
+            if level + 1 < levels:
+                first_send(level + 1, b)
+                sum_send(level + 1, b)
 
     @pl.when(s == 0)
     def _():
         for b in range(clips):
             fst[b] = xm[b * frames]
 
-    first_send(0)
-    for b in range(clips):
+    for b in range(clips):
+        first_send(0, b)
         total = cotp[b, 0].astype(F32)
         for t in range(1, frames):
             total += cotp[b, t].astype(F32)
         csum[b] = total
-    sum_send(0)
+        sum_send(0, b)
 
     @pl.when(s == n - 1)
     def _():
@@ -181,27 +196,27 @@
         dst[bt, span, chans:2 * chans] = value
         dst[bt, span, 2 * chans:3 * chans] = hi
 
-    def spread_own(dst, src, flip):
-        @pl.loop(0, clips * frames)
+    def spread_own(dst, src, flip, begin, end):
+        @pl.loop(begin, end)
         def _(bt):
             for r in range(rows):
                 spread(dst, bt, r + 1, src[bt, r * cols:(r + 1) * cols], flip)
 
-    def spread_halo(dst, src, flip):
-        @pl.loop(0, clips * frames)
+    def spread_halo(dst, src, flip, begin, end):
+        @pl.loop(begin, end)
         def _(bt):
             got = src[bt].astype(F32)
             spread(dst, bt, 0, (got * c.astype(F32)).astype(BF), flip)
             spread(dst, bt, rows + 1, (got * (1 - c).astype(F32)).astype(BF), flip)
 
-    spread_own(x3, xm, False)
+    spread_own(x3, xm, False, 0, clips * frames)
 
     @pl.loop(0, clips * frames)
     def _(bt):
         xt[bt] = xm[bt].T
 
     x_halo.wait()
-    spread_halo(x3, xh, False)
+    spread_halo(x3, xh, False, 0, clips * frames)
 
     for b in range(clips):
         @pl.loop(0, frames)
@@ -215,37 +230,7 @@
             actp[b, frames + t] = act
             at[bt] = act.T
 
-    first_recv(0)
-    if levels > 1:
-        first_send(1)
-    sum_recv(0)
-    if levels > 1:
-        sum_send(1)
-
-    for b in range(clips):
-        @pl.when(s < n - 1)
-        def _():
-            cot_copy(b).wait_recv()
-
-        @pl.when(s < n - 1)
-        def _():
-            act_copy(b).start()
-
-        @pl.loop(0, frames)
-        def _(t):
-            bt = b * frames + t
-            dact = nt(cotp[b, t], tw[0])
-            for k in range(1, 3):
-                dact += nt(cotp[b, t + k], tw[k])
-            value = pre[bt]
-            sig = jax.nn.sigmoid(value)
-            dm[bt] = (dact * sig * (1.0 + value * (1.0 - sig))).astype(BF)
-
-    d_halo.start()
-    for level in range(1, levels):
-        first_recv(level)
-        if level + 1 < levels:
-            first_send(level + 1)
+    serve(1)
 
     base = [sum(sizes[:k]) for k in range(len(sizes))]
 
@@ -339,117 +324,164 @@
     def stage_end(k):
         tg_copy(k, 1 - c).wait_recv()
 
-    def write_tap(k, tap, value):
-        acc[base[k] + tap * chans:base[k] + (tap + 1) * chans] = value
-
-    for b in range(clips):
-        ft[b] = fst[b].T
-    for k in range(3):
-        total = jnp.zeros((chans, chans), F32)
-        for b in range(clips):
-            for t in range(frames):
-                total += nn(at[b * frames + t], cotp[b, t + k])
-        write_tap(0, k, total)
-    total = jnp.zeros((chans, chans), F32)
-    for b in range(clips):
-        for t in range(frames):
-            total += nn(ft[b], cotp[b, t])
-    write_tap(0, 3, total)
-    for k in range(4):
-        used = (4 if k == 0 else 3) * chans
-        if sizes[k] > used:
-            acc[base[k] + used:base[k] + sizes[k]] = jnp.zeros((sizes[k] - used, chans), F32)
-    tm_copy(0).start()
-
-    spread_own(d3, dm, True)
-    d_halo.wait()
-    spread_halo(d3, dh, True)
-    stage_x(0)
-
-    def spatial_grad(i):
+    def add_tap(k, tap, value, b):
+        span = slice(base[k] + tap * chans, base[k] + (tap + 1) * chans)
+        if b == 0:
+            acc[span] = value
+        else:
+            acc[span] += value
+
+    for k, taps in enumerate((3, 3, 3, 3, 1)):
+        if sizes[k] > taps * chans:
+            acc[base[k] + taps * chans:base[k] + sizes[k]] = jnp.zeros(
+                (sizes[k] - taps * chans, chans), F32)
+
+    def spatial_grad(b, i):
         for j in range(3):
             total = jnp.zeros((chans, chans), F32)
-            for bt in range(clips * frames):
+            for bt in range(b * frames, (b + 1) * frames):
                 piece = d3[bt, (2 - i) * cols:(2 - i) * cols + pos, j * chans:(j + 1) * chans]
                 total += nn(xt[bt], piece)
-            write_tap(1 + i, j, total)
-        tm_copy(1 + i).start()
-
-    spatial_grad(0)
-    stage_z(0)
-    spatial_grad(1)
-    stage_x(1)
-    spatial_grad(2)
-    stage_x(2)
-    stage_z(1)
-    stage_x(3)
-    stage_g(0)
-    stage_z(2)
-
-    for level in range(1, levels):
-        sum_recv(level)
-        if level + 1 < levels:
-            sum_send(level + 1)
-
-    @pl.when(s == 0)
-    def _():
-        for b in range(clips):
-            high = csum[b].astype(BF)
-            low = (csum[b] - high.astype(F32)).astype(BF)
-            cb[b] = nt(high, cw[...]) + nt(low, cw[...])
-
-    @pl.when(s > 0)
-    def _():
-        cb[...] = jnp.zeros((clips, pos, chans), F32)
-
-    def back(b, t):
+            add_tap(1 + i, j, total, b)
+
+    def back_sum(b, t):
         bt = b * frames + t
         total = cotp[b, t].astype(F32)
         for i in range(3):
             for j in range(3):
                 piece = d3[bt, (2 - i) * cols:(2 - i) * cols + pos, j * chans:(j + 1) * chans]
                 total += nt(piece, sw[i, j * chans:(j + 1) * chans])
-        if t == 0:
-            total += cb[b]
-        glat[b, t] = (total * mask_of(b, t)).astype(BF)
-
+        return total
+
+    for b in range(clips):
+        @pl.when(s < n - 1)
+        def _():
+            cot_copy(b).wait_recv()
+
+        if b == clips - 1:
+            @pl.when(s < n - 1)
+            def _():
+                for each in range(clips):
+                    act_copy(each).start()
+
+        @pl.loop(0, frames)
+        def _(t):
+            bt = b * frames + t
+            dact = nt(cotp[b, t], tw[0])
+            for k in range(1, 3):
+                dact += nt(cotp[b, t + k], tw[k])
+            value = pre[bt]
+            sig = jax.nn.sigmoid(value)
+            dm[bt] = (dact * sig * (1.0 + value * (1.0 - sig))).astype(BF)
+
+        d_halo(b).start()
+        for k in range(3):
+            total = jnp.zeros((chans, chans), F32)
+            for t in range(frames):
+                total += nn(at[b * frames + t], cotp[b, t + k])
+            add_tap(0, k, total, b)
+        if b == clips - 1:
+            tm_copy(0).start()
+        spread_own(d3, dm, True, b * frames, (b + 1) * frames)
+        d_halo(b).wait()
+        spread_halo(d3, dh, True, b * frames, (b + 1) * frames)
+        if b < clips - 1:
+            for i in range(3):
+                spatial_grad(b, i)
+            serve(2)
+
+    last = clips - 1
+    stage_x(0)
+    spatial_grad(last, 0)
+    tm_copy(1).start()
+    spatial_grad(last, 1)
+    tm_copy(2).start()
+    stage_x(1)
+    spatial_grad(last, 2)
+    tm_copy(3).start()
+    stage_x(2)
+    stage_z(0)
+    stage_x(3)
+    serve(2)
+
+    for b in range(clips):
+        for t in range(1, frames):
+            glat[b, t] = (back_sum(b, t) * mask_of(b, t)).astype(BF)
+        if b == 0:
+            stage_z(1)
+            stage_g(0)
+    stage_z(2)
+    stage_g(1)
     stage_z(3)
-    stage_g(1)
-    for b in range(clips):
-        for t in range(frames):
-            back(b, t)
+    for b in range(clips):
+        pre[b] = back_sum(b, 0)
     stage_xg(0)
     stage_g(2)
     stage_g(3)
     stage_xg(1)
+    serve(len(hops))
+
+    total = jnp.zeros((chans, chans), F32)
+    for b in range(clips):
+        ft[b] = fst[b].T
+        for t in range(frames):
+            total += nn(ft[b], cotp[b, t])
+    add_tap(4, 0, total, 0)
+    tm_copy(4).start()
+
+    @pl.when(s == 0)
+    def _():
+        for b in range(clips):
+            high = csum[b].astype(BF)
+            low = (csum[b] - high.astype(F32)).astype(BF)
+            pre[b] += nt(high, cw[...]) + nt(low, cw[...])
+
+    for b in range(clips):
+        glat[b, 0] = (pre[b] * mask_of(b, 0)).astype(BF)
+    stage_x(4)
     stage_tg(0)
-
-    for b in range(clips):
-        @pl.when(s > 0)
-        def _():
-            act_copy(b).wait_recv()
+    stage_xg(2)
+
+    for b in range(clips):
         cond = nn(fst[b], cw[...])
         for t in range(frames):
-            total = xm[b * frames + t].astype(F32) + cond
-            for k in range(3):
+            bt = b * frames + t
+            total = xm[bt].astype(F32) + cond
+            for k in range(t + 1):
+                total += nn(actp[b, frames + t - k], tw[k])
+            pre[bt] = total
+        if b == 0:
+            stage_z(4)
+    stage_xg(3)
+    stage_tg(1)
+    stage_g(4)
+    for b in range(clips):
+        @pl.when(s > 0)
+        def _():
+            act_copy(b).wait_recv()
+
+        for t in range(frames):
+            bt = b * frames + t
+            total = pre[bt]
+            for k in range(t + 1, 3):
                 total += nn(actp[b, frames + t - k], tw[k])
             out[b, t] = (total * mask_of(b, t)).astype(BF)
 
-    stage_xg(2)
-    stage_tg(1)
-    stage_xg(3)
     stage_tg(2)
+    stage_xg(4)
     stage_tg(3)
-    for k in range(4):
+    stage_tg(4)
+    for k in range(5):
         stage_end(k)
     gtm[...] = res[0:3 * chans]
-    gcd[...] = res[3 * chans:4 * chans]
+    gcd[...] = res[base[4]:base[4] + chans]
     for i in range(3):
         gsp[i * 3 * chans:(i + 1) * 3 * chans] = res[base[1 + i]:base[1 + i] + 3 * chans]
 
     for level in range(levels):
-        first_done(level)
-        sum_done(level)
+        for b in range(clips):
+            first_done(level, b)
+            sum_done(level, b)
 
     @pl.when(s > 0)
     def _():
@@ -461,7 +493,7 @@
         for b in range(clips):
             act_copy(b).wait_send()
 
-    for k in range(4):
+    for k in range(5):
         tm_copy(k).wait_send()
         x_copy(k).wait_send()
         for d in range(1, half):
@@ -480,7 +512,7 @@
     scale = (clips * frames * rows * cols * n * lax.axis_size("tm")) ** (-0.5)
     pos = rows * cols
     unit = 32 * n
-    sizes = [-(-taps * chans // unit) * unit for taps in (4, 3, 3, 3)]
+    sizes = [-(-taps * chans // unit) * unit for taps in (3, 3, 3, 3, 1)]
     total = sum(sizes)
     bt = clips * frames
     levels = len(bits_of(n))
@@ -512,9 +544,10 @@
         pltpu.VMEM((total // 4, chans), BF),
         pltpu.VMEM((half - 1, total // (2 * n), chans), BF),
         pltpu.VMEM((total, chans), BF),
-        dma((2, 2)), dma((2, clips)), dma((2, clips)), dma((2, levels)), dma((2, levels)),
-        dma((2, 4)), dma((2, 4)), dma((4, half - 1)), dma((4, half - 1)),
-        dma((4, half - 1)), dma((4, half - 1)), dma((2, 4)), dma((2, 4)),
+        dma((2, 1 + clips)), dma((2, clips)), dma((2, clips)),
+        dma((2, levels, clips)), dma((2, levels, clips)),
+        dma((2, 5)), dma((2, 5)), dma((5, half - 1)), dma((5, half - 1)),
+        dma((5, half - 1)), dma((5, half - 1)), dma((2, 5)), dma((2, 5)),
     ]
     vmem = pl.BlockSpec(memory_space=pltpu.VMEM)
     smem = pl.BlockSpec(memory_space=pltpu.SMEM)

time: 139 us -> 125 us (0.90)
  Pallas kernels: 130 us -> 116 us
    pallas_call x1, Pallas kernels: 130 us -> 116 us  [on_device(): pl.pallas_call(functools.partial(kernel, n, (clips, frames, rows, cols, c...]
where the time goes in v3:
time: 125 us
  Pallas kernels  116 us (93%)
  local copies, waits for them, and re-layouts  7.23 us (6%)
    pallas_call x1, Pallas kernels, on_device(): pl.pallas_call(functools.partial(kernel, n, (clips, frames, rows, cols, c...  116 us
    unnamed x13, local copies, waits for them, and re-layouts  6.64 us

profile of v3, /device:TPU:0, one launch (start us, length us, event | category | flops | bytes accessed | tf_op | source)
XLA Modules:
  0.0 124.6 jit_solution(14465191683609925442)
XLA Ops:
  0.6 0.7 compare_convert_fusion
  1.4 0.6 reshape.49.refs_2_
  2.0 115.9 %shard_map.101 = (bf16[2,2,512,256]{3,2,1,0:T(8,128)(2,1)}, bf16[2,2,512,256]{3,2,1,0:T(8,128)(2,1)}, bf16[2304,256]{1,0:T(8,128)(2,1)}, bf16[768,256]{1,0:T(8,128)(2,1)}, bf16[256,256]{1,0:T(8,128)(2,1)}) custom-call(bf16[2,2,512,256]{3,2,1,0:T(8,128)(2,1)} %bitcast.11, bf16[2,2,512,256]{3,2,1,0:T(8,128)(2,1)} %bitcast.12, f32[4]{0:T(128)} %reshape.49.refs_2_, ...), custom_call_target="tpu_custom_call" | custom-call | tf_op jit(solution)/shard_map/pallas_call | solution.py:555
  117.9 0.0 copy-start.1
  117.9 2.4 %copy.16 = bf16[2,2,2,256,256]{4,3,2,1,0:T(8,128)(2,1)} copy(bf16[2,2,2,256,256]{4,3,2,1,0:T(8,128)(2,1)} %bitcast.10) | data formatting | bytes 2097152
  120.3 0.0 copy-done.1
  120.3 0.0 copy-start
  120.3 1.0 copy.17
  121.2 0.7 copy-done
  121.9 0.0 copy-start.2
  121.9 0.0 copy-start.3
  121.9 1.0 copy.18
  122.9 0.2 copy-done.2
  123.1 0.7 copy.19
  123.9 0.0 copy-done.3
  123.9 0.7 copy.20
  (1 shorter events, 0.0 us)
Async XLA Ops:
  117.9 2.4 %copy-start.1 = (bf16[2,2,512,256]{3,2,1,0:T(8,128)(2,1)S(1)}, bf16[2,2,512,256]{3,2,1,0:T(8,128)(2,1)}, u32[]{:S(2)}) copy-start(bf16[2,2,512,256]{3,2,1,0:T(8,128)(2,1)} %get-tuple-element.11) | copy-start | bytes 3145732
  120.3 1.6 %copy-start = (bf16[2304,256]{1,0:T(8,128)(2,1)S(1)}, bf16[2304,256]{1,0:T(8,128)(2,1)}, u32[]{:S(2)}) copy-start(bf16[2304,256]{1,0:T(8,128)(2,1)} %get-tuple-element.12) | copy-start | bytes 3538948
  121.9 1.2 copy-start.2
  121.9 2.0 %copy-start.3 = (bf16[256,256]{1,0:T(8,128)(2,1)S(1)}, bf16[256,256]{1,0:T(8,128)(2,1)}, u32[]{:S(2)}) copy-start(bf16[256,256]{1,0:T(8,128)(2,1)} %get-tuple-element.24) | copy-start | bytes 393220

commit v4 on v3

--- a/solution.py
+++ b/solution.py
@@ -33,9 +33,9 @@
     clips, frames, rows, cols, chans, sizes = dims
     (lat, cotan, mask, sw, tw, cw, out, glat, gsp, gtm, gcd,
      xm, xh, x3, xt, pre, actp, at, cotp, dm, dh, fst, ft, csum, cs, cr, cb,
-     acc, tmr, xs, xr, ms, zs, zr, res,
+     acc, tmr, xs, xr, zs, zr, res, swt, twt,
      halo_sem, cot_sem, act_sem, first_sem, sum_sem, tm_sem, x_sem, z_send, z_recv,
-     g_send, g_recv, xg_sem, tg_sem) = refs
+     g_send, g_recv, tg_sem) = refs
     d3 = x3
     group = lax.axis_index("groups")
     s = lax.axis_index("space")
@@ -232,93 +232,79 @@
 
     serve(1)
 
+    for k in range(3):
+        twt[k] = tw[k].T
+        for j in range(3):
+            span = slice(j * chans, (j + 1) * chans)
+            swt[k, span] = sw[k, span].T
+
     base = [sum(sizes[:k]) for k in range(len(sizes))]
 
-    def part(k, div, index, count):
-        size = sizes[k] // div
-        return pl.ds(pl.multiple_of(index * size, 16), size * count)
-
-    def shift(k, div, offset):
-        size = sizes[k] // div
-        return pl.ds(pl.multiple_of(base[k] // div + offset, 16), size)
+    def rows_at(start, size):
+        return pl.ds(pl.multiple_of(start, 16), size)
 
     def tm_copy(k):
         size = sizes[k] // 2
-        src = acc.at[pl.ds(pl.multiple_of(base[k] + (1 - c) * size, 16), size)]
+        src = acc.at[rows_at(base[k] + (1 - c) * size, size)]
         return copy(src, tmr.at[pl.ds(base[k] // 2, size)], pair(tm_sem, k), partner)
-
-    def x_copy(k):
-        span = pl.ds(base[k] // 4, sizes[k] // 4)
-        return copy(xs.at[span], xr.at[span], pair(x_sem, k), side)
 
     def z_peer(d):
         other = lax.rem(q + d, half)
         return other, at_dev(2 * other + xb, c)
 
     def z_copy(k, d):
-        size = sizes[k] // (2 * n)
+        size = sizes[k] // n
         other, dev = z_peer(d)
-        src = zs.at[pl.ds(pl.multiple_of(base[k] // 4 + other * size, 16), size)]
-        dst = zr.at[d - 1, pl.ds(base[k] // (2 * n), size)]
+        src = zs.at[rows_at(base[k] // 2 + other * size, size)]
+        dst = zr.at[d - 1, pl.ds(base[k] // n, size)]
         return copy(src, dst, (z_send.at[k, d - 1], z_recv.at[k, d - 1]), dev)
 
-    def quarter(k):
-        return base[k] + c * (sizes[k] // 2) + xb * (sizes[k] // 4)
+    def x_copy(k):
+        span = pl.ds(base[k] // n, sizes[k] // n)
+        return copy(xs.at[span], xr.at[span], pair(x_sem, k), side)
 
     def g_copy(k, d, place):
-        size = sizes[k] // (2 * n)
-        own = res.at[pl.ds(pl.multiple_of(quarter(k) + place * size, 16), size)]
+        size = sizes[k] // n
+        own = res.at[rows_at(base[k] + c * (sizes[k] // 2) + place * size, size)]
         return copy(own, own, (g_send.at[k, d - 1], g_recv.at[k, d - 1]), z_peer(d)[1])
-
-    def xg_copy(k, bit):
-        size = sizes[k] // 4
-        start = base[k] + c * (sizes[k] // 2) + bit * size
-        own = res.at[pl.ds(pl.multiple_of(start, 16), size)]
-        return copy(own, own, pair(xg_sem, k), side)
 
     def tg_copy(k, bit):
         size = sizes[k] // 2
-        own = res.at[pl.ds(pl.multiple_of(base[k] + bit * size, 16), size)]
+        own = res.at[rows_at(base[k] + bit * size, size)]
         return copy(own, own, pair(tg_sem, k), partner)
 
-    def stage_x(k):
+    def stage_z(k):
         tm_copy(k).wait_recv()
-        size = sizes[k] // 4
-        away = (1 - xb) * size
-        xs[pl.ds(base[k] // 4, size)] = (
-            acc[pl.ds(pl.multiple_of(base[k] + c * 2 * size + away, 16), size)]
-            + tmr[pl.ds(pl.multiple_of(base[k] // 2 + away, 16), size)]).astype(BF)
-        x_copy(k).start()
-
-    def stage_z(k):
-        x_copy(k).wait_recv()
-        size = sizes[k] // 4
-        span = pl.ds(base[k] // 4, size)
-        total = (acc[pl.ds(pl.multiple_of(quarter(k), 16), size)]
-                 + tmr[pl.ds(pl.multiple_of(base[k] // 2 + xb * size, 16), size)]
-                 + xr[span].astype(F32))
-        ms[span] = total
+        size = sizes[k] // 2
+        span = pl.ds(base[k] // 2, size)
+        total = acc[rows_at(base[k] + c * size, size)] + tmr[span]
+        tmr[span] = total
         zs[span] = total.astype(BF)
         for d in range(1, half):
             z_copy(k, d).start()
 
-    def stage_g(k):
-        size = sizes[k] // (2 * n)
-        total = ms[pl.ds(pl.multiple_of(base[k] // 4 + q * size, 16), size)]
+    def stage_x(k):
+        size = sizes[k] // n
+        span = pl.ds(base[k] // n, size)
+        total = tmr[rows_at(base[k] // 2 + q * size, size)]
         for d in range(1, half):
             z_copy(k, d).wait_recv()
-            total += zr[d - 1, pl.ds(base[k] // (2 * n), size)].astype(F32)
-        res[pl.ds(pl.multiple_of(quarter(k) + q * size, 16), size)] = (total * scale).astype(BF)
+            total += zr[d - 1, span].astype(F32)
+        xs[span] = total.astype(BF)
+        x_copy(k).start()
+
+    def stage_g(k):
+        size = sizes[k] // n
+        span = pl.ds(base[k] // n, size)
+        x_copy(k).wait_recv()
+        total = xs[span].astype(F32) + xr[span].astype(F32)
+        res[rows_at(base[k] + c * (sizes[k] // 2) + q * size, size)] = (total * scale).astype(BF)
         for d in range(1, half):
             g_copy(k, d, q).start()
 
-    def stage_xg(k):
+    def stage_tg(k):
         for d in range(1, half):
             g_copy(k, d, lax.rem(q + half - d, half)).wait_recv()
-        xg_copy(k, xb).start()
-
-    def stage_tg(k):
-        xg_copy(k, 1 - xb).wait_recv()
         tg_copy(k, c).start()
 
     def stage_end(k):
@@ -348,9 +334,7 @@
         bt = b * frames + t
         total = cotp[b, t].astype(F32)
         for i in range(3):
-            for j in range(3):
-                piece = d3[bt, (2 - i) * cols:(2 - i) * cols + pos, j * chans:(j + 1) * chans]
-                total += nt(piece, sw[i, j * chans:(j + 1) * chans])
+            total += nn(d3[bt, (2 - i) * cols:(2 - i) * cols + pos], swt[i])
         return total
 
     for b in range(clips):
@@ -358,6 +342,8 @@
         def _():
             cot_copy(b).wait_recv()
 
+        if b == 0:
+            serve(2)
         if b == clips - 1:
             @pl.when(s < n - 1)
             def _():
@@ -367,9 +353,9 @@
         @pl.loop(0, frames)
         def _(t):
             bt = b * frames + t
-            dact = nt(cotp[b, t], tw[0])
+            dact = nn(cotp[b, t], twt[0])
             for k in range(1, 3):
-                dact += nt(cotp[b, t + k], tw[k])
+                dact += nn(cotp[b, t + k], twt[k])
             value = pre[bt]
             sig = jax.nn.sigmoid(value)
             dm[bt] = (dact * sig * (1.0 + value * (1.0 - sig))).astype(BF)
@@ -391,34 +377,17 @@
             serve(2)
 
     last = clips - 1
-    stage_x(0)
+    stage_z(0)
     spatial_grad(last, 0)
     tm_copy(1).start()
     spatial_grad(last, 1)
     tm_copy(2).start()
-    stage_x(1)
+    stage_z(1)
     spatial_grad(last, 2)
     tm_copy(3).start()
-    stage_x(2)
-    stage_z(0)
-    stage_x(3)
-    serve(2)
-
-    for b in range(clips):
-        for t in range(1, frames):
-            glat[b, t] = (back_sum(b, t) * mask_of(b, t)).astype(BF)
-        if b == 0:
-            stage_z(1)
-            stage_g(0)
     stage_z(2)
-    stage_g(1)
+    stage_x(0)
     stage_z(3)
-    for b in range(clips):
-        pre[b] = back_sum(b, 0)
-    stage_xg(0)
-    stage_g(2)
-    stage_g(3)
-    stage_xg(1)
     serve(len(hops))
 
     total = jnp.zeros((chans, chans), F32)
@@ -434,13 +403,26 @@
         for b in range(clips):
             high = csum[b].astype(BF)
             low = (csum[b] - high.astype(F32)).astype(BF)
-            pre[b] += nt(high, cw[...]) + nt(low, cw[...])
-
-    for b in range(clips):
-        glat[b, 0] = (pre[b] * mask_of(b, 0)).astype(BF)
+            cb[b] = nt(high, cw[...]) + nt(low, cw[...])
+
+    @pl.when(s > 0)
+    def _():
+        cb[...] = jnp.zeros((clips, pos, chans), F32)
+
+    stage_x(1)
+    stage_z(4)
+    for b in range(clips):
+        for t in range(frames):
+            total = back_sum(b, t)
+            if t == 0:
+                total += cb[b]
+            glat[b, t] = (total * mask_of(b, t)).astype(BF)
+        if b == 0:
+            stage_x(2)
+            stage_g(0)
+    stage_x(3)
+    stage_g(1)
     stage_x(4)
-    stage_tg(0)
-    stage_xg(2)
 
     for b in range(clips):
         cond = nn(fst[b], cw[...])
@@ -450,10 +432,9 @@
             for k in range(t + 1):
                 total += nn(actp[b, frames + t - k], tw[k])
             pre[bt] = total
-        if b == 0:
-            stage_z(4)
-    stage_xg(3)
-    stage_tg(1)
+    stage_g(2)
+    stage_g(3)
+    stage_tg(0)
     stage_g(4)
     for b in range(clips):
         @pl.when(s > 0)
@@ -467,10 +448,8 @@
                 total += nn(actp[b, frames + t - k], tw[k])
             out[b, t] = (total * mask_of(b, t)).astype(BF)
 
-    stage_tg(2)
-    stage_xg(4)
-    stage_tg(3)
-    stage_tg(4)
+    for k in range(1, 5):
+        stage_tg(k)
     for k in range(5):
         stage_end(k)
     gtm[...] = res[0:3 * chans]
@@ -499,8 +478,16 @@
         for d in range(1, half):
             z_copy(k, d).wait_send()
             g_copy(k, d, q).wait_send()
-        xg_copy(k, xb).wait_send()
         tg_copy(k, c).wait_send()
+
+
+def hand_over(*refs):
+    sems = refs[10]
+    copies = [pltpu.make_async_copy(refs[i], refs[5 + i], sems.at[i]) for i in range(5)]
+    for each in copies:
+        each.start()
+    for each in copies:
+        each.wait()
 
 
 def on_device(latents, cotangent, valid_frames, spatial_weight, temporal_weight, cond_weight):
@@ -511,7 +498,7 @@
     mask = (frame_ids[None, :] < valid_frames[:, None]).astype(F32).reshape(clips * frames)
     scale = (clips * frames * rows * cols * n * lax.axis_size("tm")) ** (-0.5)
     pos = rows * cols
-    unit = 32 * n
+    unit = 16 * n
     sizes = [-(-taps * chans // unit) * unit for taps in (3, 3, 3, 3, 1)]
     total = sum(sizes)
     bt = clips * frames
@@ -538,16 +525,17 @@
         pltpu.VMEM((clips, pos, chans), F32),
         pltpu.VMEM((total, chans), F32),
         pltpu.VMEM((total // 2, chans), F32),
-        pltpu.VMEM((total // 4, chans), BF),
-        pltpu.VMEM((total // 4, chans), BF),
-        pltpu.VMEM((total // 4, chans), F32),
-        pltpu.VMEM((total // 4, chans), BF),
-        pltpu.VMEM((half - 1, total // (2 * n), chans), BF),
+        pltpu.VMEM((total // n, chans), BF),
+        pltpu.VMEM((total // n, chans), BF),
+        pltpu.VMEM((total // 2, chans), BF),
+        pltpu.VMEM((half - 1, total // n, chans), BF),
         pltpu.VMEM((total, chans), BF),
+        pltpu.VMEM((3, 3 * chans, chans), BF),
+        pltpu.VMEM((3, chans, chans), BF),
         dma((2, 1 + clips)), dma((2, clips)), dma((2, clips)),
         dma((2, levels, clips)), dma((2, levels, clips)),
         dma((2, 5)), dma((2, 5)), dma((5, half - 1)), dma((5, half - 1)),
-        dma((5, half - 1)), dma((5, half - 1)), dma((2, 5)), dma((2, 5)),
+        dma((5, half - 1)), dma((5, half - 1)), dma((2, 5)),
     ]
     vmem = pl.BlockSpec(memory_space=pltpu.VMEM)
     smem = pl.BlockSpec(memory_space=pltpu.SMEM)
@@ -565,6 +553,14 @@
     )(
         latents.reshape(big), cotangent.reshape(big), mask,
         spatial_weight.reshape(3, 3 * chans, chans), temporal_weight, cond_weight)
+    anywhere = pl.BlockSpec(memory_space=pl.ANY)
+    outs = pl.pallas_call(
+        hand_over,
+        out_shape=[shape(one.shape, one.dtype) for one in outs],
+        in_specs=[anywhere] * 5,
+        out_specs=[anywhere] * 5,
+        scratch_shapes=[dma((5,))],
+    )(*outs)
     output, grad_latents, grad_spatial, grad_temporal, grad_cond = outs
     return (
         output.reshape(latents.shape), grad_latents.reshape(latents.shape),

time: 125 us -> 237 us (1.90); the launches traced: 125 us -> 234 us
  Pallas kernels: 116 us -> 231 us
  local copies, waits for them, and re-layouts: 7.23 us -> 0.59 us
    pallas_call x0 -> x1, Pallas kernels: none -> 116 us  [on_device(): pl.pallas_call(hand_over, out_shape=[shape(one.shape, one.dtype) for one...]
    unnamed x13 -> x0, local copies, waits for them, and re-layouts: 6.64 us -> none
where the time goes in v4:
time: 237 us; the launch traced here: 234 us
  Pallas kernels  231 us (97%)
    pallas_call x1, Pallas kernels, on_device(): pl.pallas_call(hand_over, out_shape=[shape(one.shape, one.dtype) for one...  116 us
    pallas_call x1, Pallas kernels, on_device(): pl.pallas_call(functools.partial(kernel, n, (clips, frames, rows, cols, c...  115 us

profile of v4, /device:TPU:0, one launch (start us, length us, event | category | flops | bytes accessed | tf_op | source)
XLA Modules:
  0.0 233.5 jit_solution(17854278486430269457)
XLA Ops:
  0.6 0.7 compare_convert_fusion
  1.4 0.6 reshape.49.refs_2_
  2.0 115.1 %shard_map.101 = (bf16[2,2,512,256]{3,2,1,0:T(8,128)(2,1)}, bf16[2,2,512,256]{3,2,1,0:T(8,128)(2,1)}, bf16[2304,256]{1,0:T(8,128)(2,1)}, bf16[768,256]{1,0:T(8,128)(2,1)}, bf16[256,256]{1,0:T(8,128)(2,1)}) custom-call(bf16[2,2,512,256]{3,2,1,0:T(8,128)(2,1)} %bitcast.8, bf16[2,2,512,256]{3,2,1,0:T(8,128)(2,1)} %bitcast.9, f32[4]{0:T(128)} %reshape.49.refs_2_, ...), custom_call_target="tpu_custom_call" | custom-call | tf_op jit(solution)/shard_map/pallas_call | solution.py:543
  117.1 116.3 %shard_map.102 = (bf16[2,2,512,256]{3,2,1,0:T(8,128)(2,1)}, bf16[2,2,512,256]{3,2,1,0:T(8,128)(2,1)}, bf16[2304,256]{1,0:T(8,128)(2,1)}, bf16[768,256]{1,0:T(8,128)(2,1)}, bf16[256,256]{1,0:T(8,128)(2,1)}) custom-call(bf16[2,2,512,256]{3,2,1,0:T(8,128)(2,1)} %get-tuple-element.15.refs_0_, bf16[2,2,512,256]{3,2,1,0:T(8,128)(2,1)} %get-tuple-element.16.refs_1_, ...), custom_call_target="tpu_custom_call" | custom-call | tf_op jit(solution)/shard_map/pallas_call | solution.py:557
  (1 shorter events, 0.0 us)

commit v5 on v4

--- a/solution.py
+++ b/solution.py
@@ -34,8 +34,8 @@
     (lat, cotan, mask, sw, tw, cw, out, glat, gsp, gtm, gcd,
      xm, xh, x3, xt, pre, actp, at, cotp, dm, dh, fst, ft, csum, cs, cr, cb,
      acc, tmr, xs, xr, zs, zr, res, swt, twt,
-     halo_sem, cot_sem, act_sem, first_sem, sum_sem, tm_sem, x_sem, z_send, z_recv,
-     g_send, g_recv, tg_sem) = refs
+     halo_sem, cot_sem, act_sem, first_sem, sum_sem, tm_sem, x_sem, z_sem,
+     g_sem, tg_sem) = refs
     d3 = x3
     group = lax.axis_index("groups")
     s = lax.axis_index("space")
@@ -158,9 +158,13 @@
         for _ in range(min(count, len(hops))):
             level, b = hops.pop(0)
             first_recv(level, b)
+            if level + 1 < levels:
+                first_send(level + 1, b)
+
+    def serve_sum(level):
+        for b in range(clips):
             sum_recv(level, b)
             if level + 1 < levels:
-                first_send(level + 1, b)
                 sum_send(level + 1, b)
 
     @pl.when(s == 0)
@@ -174,7 +178,6 @@
         for t in range(1, frames):
             total += cotp[b, t].astype(F32)
         csum[b] = total
-        sum_send(0, b)
 
     @pl.when(s == n - 1)
     def _():
@@ -248,74 +251,88 @@
         src = acc.at[rows_at(base[k] + (1 - c) * size, size)]
         return copy(src, tmr.at[pl.ds(base[k] // 2, size)], pair(tm_sem, k), partner)
 
-    def z_peer(d):
-        other = lax.rem(q + d, half)
-        return other, at_dev(2 * other + xb, c)
-
-    def z_copy(k, d):
-        size = sizes[k] // n
-        other, dev = z_peer(d)
-        src = zs.at[rows_at(base[k] // 2 + other * size, size)]
-        dst = zr.at[d - 1, pl.ds(base[k] // n, size)]
-        return copy(src, dst, (z_send.at[k, d - 1], z_recv.at[k, d - 1]), dev)
+    zbits = []
+    while (1 << len(zbits)) < half:
+        zbits.append(1 << len(zbits))
+
+    def z_side(level):
+        return lax.rem(lax.div(q, zbits[level]), 2)
+
+    def z_dev(level):
+        return at_dev(s + 2 * zbits[level] * (1 - 2 * z_side(level)), c)
+
+    def kept(k, level):
+        offset = 0
+        for done in range(level):
+            offset = offset + z_side(done) * (sizes[k] >> (done + 2))
+        return offset
+
+    def z_span(k, level):
+        size = sizes[k] >> (level + 2)
+        return pl.ds(base[k] // 2 + sizes[k] // 2 - 2 * size, size)
+
+    def z_copy(k, level):
+        span = z_span(k, level)
+        return copy(zs.at[span], zr.at[span], pair(z_sem, k, level), z_dev(level))
 
     def x_copy(k):
         span = pl.ds(base[k] // n, sizes[k] // n)
         return copy(xs.at[span], xr.at[span], pair(x_sem, k), side)
 
-    def g_copy(k, d, place):
-        size = sizes[k] // n
-        own = res.at[rows_at(base[k] + c * (sizes[k] // 2) + place * size, size)]
-        return copy(own, own, (g_send.at[k, d - 1], g_recv.at[k, d - 1]), z_peer(d)[1])
+    def g_copy(k, level, mine):
+        size = sizes[k] >> (level + 2)
+        which = z_side(level) if mine else 1 - z_side(level)
+        start = base[k] + c * (sizes[k] // 2) + kept(k, level) + which * size
+        own = res.at[rows_at(start, size)]
+        return copy(own, own, pair(g_sem, k, level), z_dev(level))
 
     def tg_copy(k, bit):
         size = sizes[k] // 2
         own = res.at[rows_at(base[k] + bit * size, size)]
         return copy(own, own, pair(tg_sem, k), partner)
 
+    def z_send(k, level):
+        size = sizes[k] >> (level + 2)
+        away = base[k] // 2 + kept(k, level) + (1 - z_side(level)) * size
+        zs[z_span(k, level)] = tmr[rows_at(away, size)].astype(BF)
+        z_copy(k, level).start()
+
     def stage_z(k):
         tm_copy(k).wait_recv()
         size = sizes[k] // 2
         span = pl.ds(base[k] // 2, size)
-        total = acc[rows_at(base[k] + c * size, size)] + tmr[span]
-        tmr[span] = total
-        zs[span] = total.astype(BF)
-        for d in range(1, half):
-            z_copy(k, d).start()
-
-    def stage_x(k):
-        size = sizes[k] // n
-        span = pl.ds(base[k] // n, size)
-        total = tmr[rows_at(base[k] // 2 + q * size, size)]
-        for d in range(1, half):
-            z_copy(k, d).wait_recv()
-            total += zr[d - 1, span].astype(F32)
-        xs[span] = total.astype(BF)
-        x_copy(k).start()
+        tmr[span] += acc[rows_at(base[k] + c * size, size)]
+        z_send(k, 0)
+
+    def stage_zz(k, level):
+        z_copy(k, level - 1).wait_recv()
+        size = sizes[k] >> (level + 1)
+        span = rows_at(base[k] // 2 + kept(k, level), size)
+        tmr[span] += zr[z_span(k, level - 1)].astype(F32)
+        if level < len(zbits):
+            z_send(k, level)
+        else:
+            xs[pl.ds(base[k] // n, size)] = tmr[span].astype(BF)
+            x_copy(k).start()
 
     def stage_g(k):
         size = sizes[k] // n
         span = pl.ds(base[k] // n, size)
         x_copy(k).wait_recv()
         total = xs[span].astype(F32) + xr[span].astype(F32)
-        res[rows_at(base[k] + c * (sizes[k] // 2) + q * size, size)] = (total * scale).astype(BF)
-        for d in range(1, half):
-            g_copy(k, d, q).start()
-
-    def stage_tg(k):
-        for d in range(1, half):
-            g_copy(k, d, lax.rem(q + half - d, half)).wait_recv()
-        tg_copy(k, c).start()
+        start = base[k] + c * (sizes[k] // 2) + kept(k, len(zbits))
+        res[rows_at(start, size)] = (total * scale).astype(BF)
+        g_copy(k, len(zbits) - 1, True).start()
+
+    def stage_gg(k, level):
+        g_copy(k, level, False).wait_recv()
+        if level > 0:
+            g_copy(k, level - 1, True).start()
+        else:
+            tg_copy(k, c).start()
 
     def stage_end(k):
         tg_copy(k, 1 - c).wait_recv()
-
-    def add_tap(k, tap, value, b):
-        span = slice(base[k] + tap * chans, base[k] + (tap + 1) * chans)
-        if b == 0:
-            acc[span] = value
-        else:
-            acc[span] += value
 
     for k, taps in enumerate((3, 3, 3, 3, 1)):
         if sizes[k] > taps * chans:
@@ -323,12 +340,18 @@
                 (sizes[k] - taps * chans, chans), F32)
 
     def spatial_grad(b, i):
-        for j in range(3):
+        @pl.loop(0, 3)
+        def _(j):
             total = jnp.zeros((chans, chans), F32)
             for bt in range(b * frames, (b + 1) * frames):
-                piece = d3[bt, (2 - i) * cols:(2 - i) * cols + pos, j * chans:(j + 1) * chans]
+                piece = d3[bt, (2 - i) * cols:(2 - i) * cols + pos,
+                           pl.ds(pl.multiple_of(j * chans, chans), chans)]
                 total += nn(xt[bt], piece)
-            add_tap(1 + i, j, total, b)
+            span = pl.ds(pl.multiple_of(base[1 + i] + j * chans, chans), chans)
+            if b == 0:
+                acc[span] = total
+            else:
+                acc[span] += total
 
     def back_sum(b, t):
         bt = b * frames + t
@@ -342,13 +365,14 @@
         def _():
             cot_copy(b).wait_recv()
 
-        if b == 0:
-            serve(2)
         if b == clips - 1:
             @pl.when(s < n - 1)
             def _():
                 for each in range(clips):
                     act_copy(each).start()
+
+            for each in range(clips):
+                sum_send(0, each)
 
         @pl.loop(0, frames)
         def _(t):
@@ -361,11 +385,18 @@
             dm[bt] = (dact * sig * (1.0 + value * (1.0 - sig))).astype(BF)
 
         d_halo(b).start()
-        for k in range(3):
+
+        @pl.loop(0, 3)
+        def _(k):
             total = jnp.zeros((chans, chans), F32)
             for t in range(frames):
                 total += nn(at[b * frames + t], cotp[b, t + k])
-            add_tap(0, k, total, b)
+            span = pl.ds(pl.multiple_of(k * chans, chans), chans)
+            if b == 0:
+                acc[span] = total
+            else:
+                acc[span] += total
+
         if b == clips - 1:
             tm_copy(0).start()
         spread_own(d3, dm, True, b * frames, (b + 1) * frames)
@@ -377,16 +408,27 @@
             serve(2)
 
     last = clips - 1
+    deep = len(zbits)
+
+    def middle(k):
+        for level in range(1, deep):
+            stage_zz(k, level)
+
+    def outer_gather(k):
+        for level in range(deep - 1, 0, -1):
+            stage_gg(k, level)
+
     stage_z(0)
     spatial_grad(last, 0)
     tm_copy(1).start()
+    serve(2)
     spatial_grad(last, 1)
     tm_copy(2).start()
     stage_z(1)
     spatial_grad(last, 2)
     tm_copy(3).start()
     stage_z(2)
-    stage_x(0)
+    middle(0)
     stage_z(3)
     serve(len(hops))
 
@@ -395,36 +437,35 @@
         ft[b] = fst[b].T
         for t in range(frames):
             total += nn(ft[b], cotp[b, t])
-    add_tap(4, 0, total, 0)
+    acc[base[4]:base[4] + chans] = total
     tm_copy(4).start()
-
-    @pl.when(s == 0)
-    def _():
-        for b in range(clips):
-            high = csum[b].astype(BF)
-            low = (csum[b] - high.astype(F32)).astype(BF)
-            cb[b] = nt(high, cw[...]) + nt(low, cw[...])
-
-    @pl.when(s > 0)
-    def _():
-        cb[...] = jnp.zeros((clips, pos, chans), F32)
-
-    stage_x(1)
+    middle(1)
+    stage_zz(0, deep)
     stage_z(4)
-    for b in range(clips):
-        for t in range(frames):
-            total = back_sum(b, t)
-            if t == 0:
-                total += cb[b]
-            glat[b, t] = (total * mask_of(b, t)).astype(BF)
-        if b == 0:
-            stage_x(2)
-            stage_g(0)
-    stage_x(3)
+
+    @pl.loop(0, clips)
+    def _(b):
+        for t in range(1, frames):
+            glat[b, t] = (back_sum(b, t) * mask_of(b, t)).astype(BF)
+
+    middle(2)
+    stage_zz(1, deep)
+    stage_g(0)
+    middle(3)
+    serve_sum(0)
+
+    @pl.loop(0, clips)
+    def _(b):
+        cb[b] = back_sum(b, 0)
+
+    stage_zz(2, deep)
     stage_g(1)
-    stage_x(4)
-
-    for b in range(clips):
+    stage_zz(3, deep)
+    outer_gather(0)
+    middle(4)
+
+    @pl.loop(0, clips)
+    def _(b):
         cond = nn(fst[b], cw[...])
         for t in range(frames):
             bt = b * frames + t
@@ -432,15 +473,38 @@
             for k in range(t + 1):
                 total += nn(actp[b, frames + t - k], tw[k])
             pre[bt] = total
+
     stage_g(2)
+    stage_zz(4, deep)
+    stage_gg(0, 0)
+    outer_gather(1)
     stage_g(3)
-    stage_tg(0)
+    for level in range(1, levels):
+        serve_sum(level)
     stage_g(4)
+    outer_gather(2)
+
+    @pl.when(s == 0)
+    def _():
+        @pl.loop(0, clips)
+        def _(b):
+            high = csum[b].astype(BF)
+            low = (csum[b] - high.astype(F32)).astype(BF)
+            cb[b] += nt(high, cw[...]) + nt(low, cw[...])
+
+    for b in range(clips):
+        glat[b, 0] = (cb[b] * mask_of(b, 0)).astype(BF)
+    stage_gg(1, 0)
+    outer_gather(3)
+    outer_gather(4)
+
     for b in range(clips):
         @pl.when(s > 0)
         def _():
             act_copy(b).wait_recv()
 
+    @pl.loop(0, clips)
+    def _(b):
         for t in range(frames):
             bt = b * frames + t
             total = pre[bt]
@@ -448,8 +512,8 @@
                 total += nn(actp[b, frames + t - k], tw[k])
             out[b, t] = (total * mask_of(b, t)).astype(BF)
 
-    for k in range(1, 5):
-        stage_tg(k)
+    for k in range(2, 5):
+        stage_gg(k, 0)
     for k in range(5):
         stage_end(k)
     gtm[...] = res[0:3 * chans]
@@ -475,19 +539,15 @@
     for k in range(5):
         tm_copy(k).wait_send()
         x_copy(k).wait_send()
-        for d in range(1, half):
-            z_copy(k, d).wait_send()
-            g_copy(k, d, q).wait_send()
+        for level in range(len(zbits)):
+            z_copy(k, level).wait_send()
+            g_copy(k, level, True).wait_send()
         tg_copy(k, c).wait_send()
 
 
 def hand_over(*refs):
-    sems = refs[10]
-    copies = [pltpu.make_async_copy(refs[i], refs[5 + i], sems.at[i]) for i in range(5)]
-    for each in copies:
-        each.start()
-    for each in copies:
-        each.wait()
+    for i in range(5):
+        refs[5 + i][...] = refs[i][...]
 
 
 def on_device(latents, cotangent, valid_frames, spatial_weight, temporal_weight, cond_weight):
@@ -503,7 +563,6 @@
     total = sum(sizes)
     bt = clips * frames
     levels = len(bits_of(n))
-    half = n // 2
     dma = pltpu.SemaphoreType.DMA
     big = (clips, frames, pos, chans)
     scratch = [
@@ -528,14 +587,13 @@
         pltpu.VMEM((total // n, chans), BF),
         pltpu.VMEM((total // n, chans), BF),
         pltpu.VMEM((total // 2, chans), BF),
-        pltpu.VMEM((half - 1, total // n, chans), BF),
+        pltpu.VMEM((total // 2, chans), BF),
         pltpu.VMEM((total, chans), BF),
         pltpu.VMEM((3, 3 * chans, chans), BF),
         pltpu.VMEM((3, chans, chans), BF),
         dma((2, 1 + clips)), dma((2, clips)), dma((2, clips)),
         dma((2, levels, clips)), dma((2, levels, clips)),
-        dma((2, 5)), dma((2, 5)), dma((5, half - 1)), dma((5, half - 1)),
-        dma((5, half - 1)), dma((5, half - 1)), dma((2, 5)),
+        dma((2, 5)), dma((2, 5)), dma((2, 5, levels)), dma((2, 5, levels)), dma((2, 5)),
     ]
     vmem = pl.BlockSpec(memory_space=pltpu.VMEM)
     smem = pl.BlockSpec(memory_space=pltpu.SMEM)
@@ -553,13 +611,12 @@
     )(
         latents.reshape(big), cotangent.reshape(big), mask,
         spatial_weight.reshape(3, 3 * chans, chans), temporal_weight, cond_weight)
-    anywhere = pl.BlockSpec(memory_space=pl.ANY)
     outs = pl.pallas_call(
         hand_over,
         out_shape=[shape(one.shape, one.dtype) for one in outs],
-        in_specs=[anywhere] * 5,
-        out_specs=[anywhere] * 5,
-        scratch_shapes=[dma((5,))],
+        in_specs=[vmem] * 5,
+        out_specs=[vmem] * 5,
+        compiler_params=pltpu.CompilerParams(vmem_limit_bytes=24 * 2**20),
     )(*outs)
     output, grad_latents, grad_spatial, grad_temporal, grad_cond = outs
     return (

time: 237 us -> 148 us (0.62)
  Pallas kernels: 231 us -> 139 us
  local copies, waits for them, and re-layouts: 0.59 us -> 6.2 us
    pallas_call x1, Pallas kernels: 116 us -> 2.11 us  [on_device(): pl.pallas_call(hand_over, out_shape=[shape(one.shape, one.dtype) for one...]
    pallas_call x1, Pallas kernels: 115 us -> 137 us  [on_device(): pl.pallas_call(functools.partial(kernel, n, (clips, frames, rows, cols, c...]
    unnamed x0 -> x10, local copies, waits for them, and re-layouts: none -> 5.61 us
where the time goes in v5:
time: 148 us; the launch traced here: 147 us
  Pallas kernels  139 us (94%)
  local copies, waits for them, and re-layouts  6.2 us (4%)
    pallas_call x1, Pallas kernels, on_device(): pl.pallas_call(functools.partial(kernel, n, (clips, frames, rows, cols, c...  137 us
    unnamed x10, local copies, waits for them, and re-layouts  5.61 us

profile of v5, /device:TPU:0, one launch (start us, length us, event | category | flops | bytes accessed | tf_op | source)
XLA Modules:
  0.0 146.9 jit_solution(1856182430136931370)
XLA Ops:
  0.6 0.7 compare_convert_fusion
  1.4 0.6 reshape.49.refs_2_
  2.0 137.2 %shard_map.101 = (bf16[2,2,512,256]{3,2,1,0:T(8,128)(2,1)}, bf16[2,2,512,256]{3,2,1,0:T(8,128)(2,1)}, bf16[2304,256]{1,0:T(8,128)(2,1)}, bf16[768,256]{1,0:T(8,128)(2,1)}, bf16[256,256]{1,0:T(8,128)(2,1)}) custom-call(bf16[2,2,512,256]{3,2,1,0:T(8,128)(2,1)} %bitcast.8, bf16[2,2,512,256]{3,2,1,0:T(8,128)(2,1)} %bitcast.9, f32[4]{0:T(128)} %reshape.49.refs_2_, ...), custom_call_target="tpu_custom_call" | custom-call | tf_op jit(solution)/shard_map/pallas_call | solution.py:601
  139.2 0.0 copy-start
  139.2 1.3 copy-done
  140.4 0.0 copy-start.1
  140.4 1.2 copy-done.1
  141.7 0.0 copy-start.2
  141.7 1.2 copy-done.2
  142.9 0.0 copy-start.3
  142.9 1.0 copy-done.3
  143.9 0.0 copy-start.4
  143.9 0.9 copy-done.4
  144.8 2.1 %shard_map.102 = (bf16[2,2,512,256]{3,2,1,0:T(8,128)(2,1)}, bf16[2,2,512,256]{3,2,1,0:T(8,128)(2,1)}, bf16[2304,256]{1,0:T(8,128)(2,1)}, bf16[768,256]{1,0:T(8,128)(2,1)}, bf16[256,256]{1,0:T(8,128)(2,1)}) custom-call(bf16[2,2,512,256]{3,2,1,0:T(8,128)(2,1)S(1)} %copy-done.1, bf16[2,2,512,256]{3,2,1,0:T(8,128)(2,1)S(1)} %copy-done.2, ...), custom_call_target="tpu_custom_call" | custom-call | tf_op jit(solution)/shard_map/pallas_call | solution.py:614
  (1 shorter events, 0.0 us)
Async XLA Ops:
  139.2 1.3 copy-start
  140.4 1.2 copy-start.1
  141.7 1.2 copy-start.2
  142.9 1.0 copy-start.3
  143.9 0.9 copy-start.4

commit v6 on v5

--- a/solution.py
+++ b/solution.py
@@ -178,6 +178,7 @@
         for t in range(1, frames):
             total += cotp[b, t].astype(F32)
         csum[b] = total
+        sum_send(0, b)
 
     @pl.when(s == n - 1)
     def _():
@@ -368,11 +369,8 @@
         if b == clips - 1:
             @pl.when(s < n - 1)
             def _():
-                for each in range(clips):
+                for each in range(clips - 1):
                     act_copy(each).start()
-
-            for each in range(clips):
-                sum_send(0, each)
 
         @pl.loop(0, frames)
         def _(t):
@@ -406,6 +404,8 @@
             for i in range(3):
                 spatial_grad(b, i)
             serve(2)
+            if b == 0:
+                serve_sum(0)
 
     last = clips - 1
     deep = len(zbits)
@@ -428,8 +428,15 @@
     spatial_grad(last, 2)
     tm_copy(3).start()
     stage_z(2)
+    stage_z(3)
+
+    @pl.when(s < n - 1)
+    def _():
+        act_copy(last).start()
+
+    for level in range(1, levels - 1):
+        serve_sum(level)
     middle(0)
-    stage_z(3)
     serve(len(hops))
 
     total = jnp.zeros((chans, chans), F32)
@@ -452,7 +459,6 @@
     stage_zz(1, deep)
     stage_g(0)
     middle(3)
-    serve_sum(0)
 
     @pl.loop(0, clips)
     def _(b):
@@ -479,8 +485,7 @@
     stage_gg(0, 0)
     outer_gather(1)
     stage_g(3)
-    for level in range(1, levels):
-        serve_sum(level)
+    serve_sum(levels - 1)
     stage_g(4)
     outer_gather(2)
 
@@ -543,11 +548,6 @@
             z_copy(k, level).wait_send()
             g_copy(k, level, True).wait_send()
         tg_copy(k, c).wait_send()
-
-
-def hand_over(*refs):
-    for i in range(5):
-        refs[5 + i][...] = refs[i][...]
 
 
 def on_device(latents, cotangent, valid_frames, spatial_weight, temporal_weight, cond_weight):
@@ -611,13 +611,6 @@
     )(
         latents.reshape(big), cotangent.reshape(big), mask,
         spatial_weight.reshape(3, 3 * chans, chans), temporal_weight, cond_weight)
-    outs = pl.pallas_call(
-        hand_over,
-        out_shape=[shape(one.shape, one.dtype) for one in outs],
-        in_specs=[vmem] * 5,
-        out_specs=[vmem] * 5,
-        compiler_params=pltpu.CompilerParams(vmem_limit_bytes=24 * 2**20),
-    )(*outs)
     output, grad_latents, grad_spatial, grad_temporal, grad_cond = outs
     return (
         output.reshape(latents.shape), grad_latents.reshape(latents.shape),

time: 148 us -> 130 us (0.88)
  Pallas kernels: 139 us -> 121 us
    pallas_call x1, Pallas kernels: 137 us -> 121 us  [on_device(): pl.pallas_call(functools.partial(kernel, n, (clips, frames, rows, cols, c...]
    pallas_call x1 -> x0, Pallas kernels: 2.11 us -> none  [on_device(): pl.pallas_call(hand_over, out_shape=[shape(one.shape, one.dtype) for one...]
    unnamed x10 -> x13, local copies, waits for them, and re-layouts: 5.61 us -> 6.64 us
where the time goes in v6:
time: 130 us; the launch traced here: 129 us
  Pallas kernels  121 us (93%)
  local copies, waits for them, and re-layouts  7.23 us (6%)
    pallas_call x1, Pallas kernels, on_device(): pl.pallas_call(functools.partial(kernel, n, (clips, frames, rows, cols, c...  121 us
    unnamed x13, local copies, waits for them, and re-layouts  6.64 us

profile of v6, /device:TPU:0, one launch (start us, length us, event | category | flops | bytes accessed | tf_op | source)
XLA Modules:
  0.0 129.4 jit_solution(12197794661745388481)
XLA Ops:
  0.6 0.7 compare_convert_fusion
  1.4 0.6 reshape.49.refs_2_
  2.0 120.8 %shard_map.101 = (bf16[2,2,512,256]{3,2,1,0:T(8,128)(2,1)}, bf16[2,2,512,256]{3,2,1,0:T(8,128)(2,1)}, bf16[2304,256]{1,0:T(8,128)(2,1)}, bf16[768,256]{1,0:T(8,128)(2,1)}, bf16[256,256]{1,0:T(8,128)(2,1)}) custom-call(bf16[2,2,512,256]{3,2,1,0:T(8,128)(2,1)} %bitcast.11, bf16[2,2,512,256]{3,2,1,0:T(8,128)(2,1)} %bitcast.12, f32[4]{0:T(128)} %reshape.49.refs_2_, ...), custom_call_target="tpu_custom_call" | custom-call | tf_op jit(solution)/shard_map/pallas_call | solution.py:601
  122.8 0.0 copy-start.1
  122.8 2.4 %copy.16 = bf16[2,2,2,256,256]{4,3,2,1,0:T(8,128)(2,1)} copy(bf16[2,2,2,256,256]{4,3,2,1,0:T(8,128)(2,1)} %bitcast.10) | data formatting | bytes 2097152
  125.1 0.0 copy-done.1
  125.2 0.0 copy-start
  125.2 1.0 copy.17
  126.1 0.7 copy-done
  126.8 0.0 copy-start.2
  126.8 0.0 copy-start.3
  126.8 1.0 copy.18
  127.8 0.2 copy-done.2
  128.0 0.7 copy.19
  128.8 0.0 copy-done.3
  128.8 0.7 copy.20
  (1 shorter events, 0.0 us)
Async XLA Ops:
  122.8 2.4 %copy-start.1 = (bf16[2,2,512,256]{3,2,1,0:T(8,128)(2,1)S(1)}, bf16[2,2,512,256]{3,2,1,0:T(8,128)(2,1)}, u32[]{:S(2)}) copy-start(bf16[2,2,512,256]{3,2,1,0:T(8,128)(2,1)} %get-tuple-element.11) | copy-start | bytes 3145732
  125.2 1.6 %copy-start = (bf16[2304,256]{1,0:T(8,128)(2,1)S(1)}, bf16[2304,256]{1,0:T(8,128)(2,1)}, u32[]{:S(2)}) copy-start(bf16[2304,256]{1,0:T(8,128)(2,1)} %get-tuple-element.12) | copy-start | bytes 3538948
  126.8 1.2 copy-start.2
  126.8 2.0 %copy-start.3 = (bf16[256,256]{1,0:T(8,128)(2,1)S(1)}, bf16[256,256]{1,0:T(8,128)(2,1)}, u32[]{:S(2)}) copy-start(bf16[256,256]{1,0:T(8,128)(2,1)} %get-tuple-element.24) | copy-start | bytes 393220
